TPU v7x, 32 devices: a whole 2x2x4 slice. The times are simulated.
32 devices in a mesh: row: 8 (over z, y), col: 2 (over x), tp: 2 (over core).
Axes of the slice: x: 2, y: 2, z: 4, core: 2. Of those that a mesh axis runs over, the one named last changes fastest.
Arguments:
- gram: float32 [16, 8, 128, 8, 2, 1024], P(None, 'row', 'tp', None, 'col'), may hold values from -24 to 24
- inv_factor: bfloat16 [1024, 1024], replicated, as said below
- cross_gram: bfloat16 [16, 8, 128, 1024], P(None, 'row', 'tp'), may hold values from -24 to 24
- down_rows: bfloat16 [29568, 4096], P(('row', 'tp'), 'col'), may hold values from -0.03125 to 0.03125
- removed: int32 [1024], replicated, may hold values from 0 to 29567, as said below
Outputs:
- updated: float32 [16, 8, 128, 8, 2, 1024], P(None, 'row', 'tp', None, 'col')
- rhs_next: float32 [16, 8, 128, 4096], P(None, 'row', 'tp', 'col')
Inputs may be any that keep to these rules, and one draw needn't show every extreme that they name: `inv_factor`: zero above the diagonal. `removed`: distinct ids in ascending order; among the neurons s * 1848 to (s + 1) * 1848 - 1 of any shard s at most 256 are listed, and one shard holds exactly 256.
All inputs are finite; a program needn't handle non-finite values.
Results may differ from a plain program's by a relative error of at most 0.0003.
Values may be sent and summed in bfloat16 or wider, within the bound.
No kernel may reach another device: no remote copies, remote signals or barrier semaphores. Data moves between devices by JAX's collectives and lax.ppermute only.
A program may use at most 256 MiB of HBM per device.

v0:
```python
import jax
import jax.numpy as jnp
from jax import lax
from jax.sharding import PartitionSpec as P


def broadcast(block, axis, holder):
    block = jnp.where(lax.axis_index(axis) == holder, block, jnp.zeros_like(block))
    return lax.psum(block, axis)


def per_device(gram, inv_factor, cross_gram, down_rows, removed):
    highest = lax.Precision.HIGHEST
    cycles = gram.shape[0]
    half = gram.shape[2]
    col_cycles = gram.shape[3]
    block = gram.shape[5]
    rows_local = cycles * half
    panel_width = inv_factor.shape[0]
    grid = gram.reshape(rows_local, col_cycles, block)
    factor = inv_factor.astype(jnp.float32)
    head_columns = grid[:, 0, :panel_width]
    panel = broadcast(head_columns, "col", 0)
    left = jnp.dot(panel, factor.T, precision=highest, preferred_element_type=jnp.float32)
    col_count = lax.axis_size("col")
    by_cycle = left.reshape(col_cycles, col_count, half, panel_width)
    wanted = lax.dynamic_index_in_dim(by_cycle, lax.axis_index("col"), axis=1, keepdims=False)
    product = jnp.einsum(
        "rp,cwp->rcw",
        left,
        lax.all_gather(wanted, ("row", "tp"), axis=1, tiled=True),
        precision=highest,
        preferred_element_type=jnp.float32,
    )
    updated = grid - product
    shard = down_rows.shape[0]
    count_all = removed.shape[0]
    member = lax.axis_index(("row", "tp"))
    owner = removed // shard
    capacity = 4 * count_all // lax.axis_size(("row", "tp"))
    earlier = jnp.sum(owner[None, :] < owner[:, None], axis=1)
    within = jnp.arange(count_all, dtype=jnp.int32) - earlier
    own_start = jnp.sum(owner < member)
    slot_ids = jnp.clip(own_start + jnp.arange(capacity, dtype=jnp.int32), 0, count_all - 1)
    local_ids = jnp.clip(removed[slot_ids] - member * shard, 0, shard - 1)
    packed = jnp.take(down_rows, local_ids, axis=0)
    everyone = lax.all_gather(packed, ("row", "tp"), axis=0, tiled=True)
    lost_rows = jnp.take(everyone, owner * capacity + within, axis=0)
    cross = cross_gram.reshape(rows_local, cross_gram.shape[3])
    rhs = jnp.dot(cross, lost_rows, preferred_element_type=jnp.float32)
    leading = rhs[:half]
    stacked = lax.all_gather(leading, ("row", "tp"), axis=0, tiled=True)
    solved = jnp.dot(
        factor, stacked[:panel_width], precision=highest, preferred_element_type=jnp.float32
    )
    rhs_next = rhs - jnp.dot(left, solved, precision=highest, preferred_element_type=jnp.float32)
    return (updated.reshape(gram.shape), rhs_next.reshape(cycles, 1, half, rhs.shape[1]))


def solution(mesh):
    return jax.shard_map(
        per_device,
        mesh=mesh,
        in_specs=(
            P(None, "row", "tp", None, "col", None),
            P(),
            P(None, "row", "tp", None),
            P(("row", "tp"), "col"),
            P(),
        ),
        out_specs=(P(None, "row", "tp", None, "col", None), P(None, "row", "tp", "col")),
        check_vma=False,
    )
```

profile of v0, /device:TPU:0, one launch (start us, length us, event | category | flops | bytes accessed | tf_op | source)
XLA Modules:
  0.0 577.0 jit_solution(3719397263521627103)
XLA Ops:
  8.0 0.0 copy-start
  8.0 0.0 all-gather.5.cloned.1.call-start
  8.1 1.5 convert_reduce_fusion.1
  9.5 0.7 compare_select_fusion.2
  10.2 1.9 gather_fusion
  12.2 6.5 %gather_fusion.1 = bf16[256,2048]{1,0:T(8,128)(2,1)S(1)} fusion(bf16[1848,2048]{1,0:T(8,128)(2,1)} %param.8, s32[1024]{0:T(1024)S(1)} %pad_clamp_fusion), kind=kCustom, calls=%fused_computation.1 | custom fusion | bytes 2098176 | tf_op jit(solution)/shard_map/jit(_take)/gather | solution.py:46
  18.7 1.1 broadcast_select_fusion
  19.8 0.0 all-gather.5.cloned.1.call-update
  19.8 0.0 all-reduce.2.cloned.1.call-start
  19.9 27.7 %copy.15 = f32[16,1,64,8,1,1024]{5,2,0,3,4,1:T(8,128)} copy(f32[16,1,64,8,1,1024]{5,4,3,2,1,0:T(1,128)} %param.5) | data formatting | bytes 67108864 | tf_op args[0]
  47.6 5.0 fusion.5
  52.6 0.0 all-reduce.2.cloned.1.call-update
  52.6 0.0 all-gather.7.cloned.1.call-start
  52.7 0.6 convert_reduce_fusion
  53.3 96.3 %all-gather.5.cloned.1.call-done = bf16[4096,2048]{1,0:T(8,128)(2,1)} async-done(((bf16[256,2048]{1,0:T(8,128)(2,1)}), bf16[4096,2048]{1,0:T(8,128)(2,1)}) %all-gather.5.cloned.1.call-update) | async-done | bytes 16777232 | tf_op jit(solution)/shard_map/all_gather | solution.py:47
  149.6 16.7 %gather_fusion.2 = bf16[1024,2048]{1,0:T(8,128)(2,1)} fusion(bf16[4096,2048]{1,0:T(8,128)(2,1)} %all-gather.5.cloned.1.call-done, s32[1024]{0:T(1024)S(1)} %broadcast_clamp_fusion), kind=kCustom, calls=%fused_computation.2 | custom fusion | bytes 8392704 | tf_op jit(solution)/shard_map/jit(_take)/gather | solution.py:48
  166.3 0.0 copy-done
  166.3 6.4 %convolution_bitcast_fusion = f32[1024,2048]{1,0:T(8,128)S(1)} fusion(bf16[1024,1024]{1,0:T(8,128)(2,1)S(1)} %bitcast.31, bf16[1024,2048]{1,0:T(8,128)(2,1)} %gather_fusion.2, pred[1024]{0:T(1024)(128)(4,1)S(1)} %compare_and_fusion), kind=kOutput, calls=%fused_computation.6 | convolution fusion | flops 4297064448 | bytes 14681088 | tf_op jit(solution)/shard_map/dot_general | solution.py:50
  172.8 0.0 copy-start.4
  172.8 3.4 copy-done.4
  176.2 0.8 slice.15
  177.0 0.0 all-gather.7.cloned.1.call-update
  177.0 0.3 all-gather.9.cloned.1.call-start
  177.3 0.0 all-reduce.2.cloned.1.call-done
  177.3 9.2 %fusion.12 = f32[1024,1024]{1,0:T(8,128)S(1)} fusion(f32[1024,1024]{1,0:T(8,128)} %all-reduce.2.cloned.1.call-done, bf16[1024,1024]{1,0:T(8,128)(2,1)} %param.6), kind=kOutput, calls=%fused_computation.33 | convolution fusion | flops 12884901888 | bytes 10485760 | tf_op jit(solution)/shard_map/dot_general | solution.py:24
  186.5 0.0 copy-start.2
  186.5 0.0 copy-start.5
  186.5 2.1 copy-done.2
  188.6 1.5 dynamic-slice_bitcast_fusion
  190.1 0.0 all-gather.9.cloned.1.call-update
  190.2 60.1 %all-gather.7.cloned.1.call-done = f32[1024,2048]{1,0:T(8,128)} async-done(((f32[64,2048]{1,0:T(8,128)}), f32[1024,2048]{1,0:T(8,128)}) %all-gather.7.cloned.1.call-update) | async-done | bytes 8388624 | tf_op jit(solution)/shard_map/all_gather | solution.py:52
  250.3 0.0 copy-done.5
  250.3 0.0 copy-start.3
  250.3 29.3 %fusion.13 = f32[2048,1024]{1,0:T(8,128)S(1)} fusion(f32[1024,2048]{1,0:T(8,128)} %all-gather.7.cloned.1.call-done, bf16[1024,1024]{1,0:T(8,128)(2,1)S(1)} %copy-done.5), kind=kOutput, calls=%fused_computation.34 | convolution fusion | flops 25769803776 | bytes 18874368 | tf_op jit(solution)/shard_map/dot_general | solution.py:53
  279.6 0.0 copy-done.3
  279.6 29.8 %convolution_subtract_fusion = f32[1024,2048]{1,0:T(8,128)} fusion(f32[1024,2048]{1,0:T(8,128)} %copy-done.4, f32[1024,1024]{1,0:T(8,128)S(1)} %copy-done.3, f32[2048,1024]{1,0:T(8,128)S(1)} %fusion.13), kind=kOutput, calls=%fused_computation.13 | convolution fusion | flops 25771900928 | bytes 29360128 | tf_op jit(solution)/shard_map/dot_general | solution.py:56
  309.4 108.8 %all-gather.9.cloned.1.call-done = f32[8,1,1024,1024]{3,2,0,1:T(8,128)} async-done(((f32[8,1,64,1024]{3,2,0,1:T(8,128)}), f32[8,1,1024,1024]{3,2,0,1:T(8,128)}) %all-gather.9.cloned.1.call-update) | async-done | bytes 33554448 | tf_op jit(solution)/shard_map/all_gather | solution.py:31
  418.2 112.8 %fusion.2 = f32[1024,8,1024]{2,0,1:T(8,128)} fusion(f32[1024,8,1024]{2,0,1:T(8,128)} %bitcast.33, f32[8,1,1024,1024]{3,2,0,1:T(8,128)} %all-gather.9.cloned.1.call-done, f32[1024,1024]{1,0:T(8,128)} %copy-done.2), kind=kOutput, calls=%fused_computation.5 | convolution fusion | flops 103087603712 | bytes 104857600 | tf_op jit(solution)/shard_map/rp,cwp->rcw/dot_general | solution.py:28
  531.0 0.0 copy-start.1
  531.0 38.7 %copy.17 = f32[16,1,64,8,1,1024]{5,4,3,2,1,0:T(1,128)} copy(f32[16,1,64,8,1,1024]{5,2,0,3,4,1:T(8,128)} %bitcast.34) | data formatting | bytes 67108864
  569.7 0.0 copy-done.1
  (6 shorter events, 0.0 us)
Async XLA Ops:
  8.0 158.3 %copy-start = (bf16[16,1,64,1024]{3,2,1,0:T(8,128)(2,1)S(1)}, bf16[16,1,64,1024]{3,2,1,0:T(8,128)(2,1)}, u32[]{:S(2)}) copy-start(bf16[16,1,64,1024]{3,2,1,0:T(8,128)(2,1)} %param.7) | copy-start | bytes 6291460
  8.0 141.6 %all-gather.5.cloned.1.call-start = ((), (), s32[]{:S(2)}) async-start(), calls=%async_computation.1 | async-start | bytes 17825792 | tf_op jit(solution)/shard_map/all_gather | solution.py:47
  19.8 157.5 %all-reduce.2.cloned.1.call-start = ((), (), s32[]{:S(2)}) async-start(), calls=%async_computation | async-start | bytes 8388608 | tf_op jit(solution)/shard_map/psum | solution.py:9
  52.6 197.6 %all-gather.7.cloned.1.call-start = ((), (), s32[]{:S(2)}) async-start(), calls=%async_computation.2 | async-start | bytes 8912896 | tf_op jit(solution)/shard_map/all_gather | solution.py:52
  172.8 3.4 copy-start.4
  177.0 241.2 %all-gather.9.cloned.1.call-start = ((), (), s32[]{:S(2)}) async-start(), calls=%async_computation.3 | async-start | bytes 35651584 | tf_op jit(solution)/shard_map/all_gather | solution.py:31
  186.5 2.1 copy-start.2
  186.5 63.8 %copy-start.5 = (bf16[1024,1024]{1,0:T(8,128)(2,1)S(1)}, bf16[1024,1024]{1,0:T(8,128)(2,1)}, u32[]{:S(2)}) copy-start(bf16[1024,1024]{1,0:T(8,128)(2,1)} %param.6) | copy-start | bytes 6291460
  250.3 29.4 %copy-start.3 = (f32[1024,1024]{1,0:T(8,128)S(1)}, f32[1024,1024]{1,0:T(8,128)}, u32[]{:S(2)}) copy-start(f32[1024,1024]{1,0:T(8,128)} %copy-done.2) | copy-start | bytes 12582916
  531.0 38.7 %copy-start.1 = (bf16[16,1,64,1024]{3,2,1,0:T(8,128)(2,1)S(1)}, bf16[16,1,64,1024]{3,2,1,0:T(8,128)(2,1)}, u32[]{:S(2)}) copy-start(bf16[16,1,64,1024]{3,2,1,0:T(8,128)(2,1)} %param.7) | copy-start | bytes 6291460
Sparse Core Ops, SparseCore 0:
  20.0 129.5 all-gather.4
  177.2 73.0 all-gather.6
  251.9 166.3 all-gather.8
Sparse Core Ops, SparseCore 1:
  52.7 110.3 all-reduce.1
where the time goes:
time: 586 us; the launch traced here: 577 us
  waiting for transfers between devices  265 us (45%)
  matrix products  187 us (32%)
  local copies, waits for them, and re-layouts  99.5 us (17%)
  between operations  15.5 us (3%)
  other arithmetic  8.89 us (2%)
    dot_general x1, matrix products, per_device(): jnp.einsum('rp,cwp->rcw', left, lax.all_gather(wanted, ('row', 'tp'), axi...  113 us
    all_gather x1, waiting for transfers between devices, per_device(): lax.all_gather(wanted, ('row', 'tp'), axis=1, tiled=True)  109 us
    all_gather x1, waiting for transfers between devices, per_device(): everyone = lax.all_gather(packed, ('row', 'tp'), axis=0, tiled=True)  96.3 us
    unnamed x15, local copies, waits for them, and re-layouts  73.5 us
    all_gather x1, waiting for transfers between devices, per_device(): stacked = lax.all_gather(leading, ('row', 'tp'), axis=0, tiled=True)  60.1 us
    dot_general x1, matrix products, per_device(): jnp.dot(left, solved, precision=highest, preferred_element_type=jnp.float32)  29.8 us
    dot_general x1, matrix products, per_device(): jnp.dot(factor, stacked[:panel_width], precision=highest, preferred_eleme...  29.3 us
    gather x1, local copies, waits for them, and re-layouts, per_device(): lost_rows = jnp.take(everyone, owner * capacity + within, axis=0)  16.7 us
  transfers between devices with their start and end apart: 4, of which 3 were waited for; matrix products, arithmetic and copies ran while one was open for 22% of the time, Pallas kernels for 0%

commit v1 on v0

v1 whole, which is shorter than its diff:
```python
import functools

import jax
import jax.numpy as jnp
from jax import lax
from jax.experimental import pallas as pl
from jax.experimental.pallas import tpu as pltpu
from jax.sharding import PartitionSpec as P

MEMBERS = ("far", "near", "tp")
LIMIT = 24.0
LEVELS = 32767.0
VMEM = 56 * 1024 * 1024

PIECES = ((0, 4), (4, 4))
STEP = 2


def encode(values):
    root = jnp.sqrt(jnp.abs(values)) * (LEVELS / LIMIT**0.5)
    code = jnp.clip(jnp.round(jnp.where(values < 0, -root, root)), -LEVELS, LEVELS).astype(jnp.int32)
    half = values.shape[-1] // 2
    return (code[..., :half] << 16) | (code[..., half:] & 0xFFFF)


def decode(words, factor):
    upper = (words >> 16).astype(jnp.float32)
    lower = ((words << 16) >> 16).astype(jnp.float32)
    return upper * (jnp.abs(upper) * factor), lower * (jnp.abs(lower) * factor)


def split(values):
    high = values.astype(jnp.bfloat16)
    return high, (values - high.astype(jnp.float32)).astype(jnp.bfloat16)


def solve_kernel(factor_ref, back_ref, words_ref, sh_ref, sl_ref, high_ref, low_ref):
    packed = words_ref.shape[1]
    total = None
    for half, values in enumerate(decode(words_ref[...], factor_ref[0])):
        high, low = split(values)
        lines = pl.ds(half * packed, packed)
        part = nn(high, sh_ref[lines, :]) + nn(low, sh_ref[lines, :]) + nn(high, sl_ref[lines, :])
        total = part if total is None else total + part
    high_ref[...], low_ref[...] = split(total * back_ref[0])


def square_kernel(turned_ref, high_ref, low_ref):
    high_ref[...], low_ref[...] = split(nt(turned_ref[...], turned_ref[...]))


def square(turned):
    whole = pl.BlockSpec(memory_space=pltpu.VMEM)
    return pl.pallas_call(
        square_kernel,
        out_shape=[jax.ShapeDtypeStruct(turned.shape, jnp.bfloat16)] * 2,
        in_specs=[whole],
        out_specs=[whole] * 2,
        compiler_params=pltpu.CompilerParams(vmem_limit_bytes=VMEM),
        name="square",
    )(turned)


def solve(factor, back, words, sh, sl):
    rows, packed = words.shape
    width = sh.shape[1]
    step = min(rows, 256)
    whole = pl.BlockSpec(sh.shape, lambda r: (0, 0))
    tile = pl.BlockSpec((step, width), lambda r: (r, 0))
    return pl.pallas_call(
        solve_kernel,
        out_shape=[jax.ShapeDtypeStruct((rows, width), jnp.bfloat16)] * 2,
        grid=(rows // step,),
        in_specs=[
            pl.BlockSpec(memory_space=pltpu.SMEM),
            pl.BlockSpec(memory_space=pltpu.SMEM),
            pl.BlockSpec((step, packed), lambda r: (r, 0)),
            whole,
            whole,
        ],
        out_specs=[tile, tile],
        compiler_params=pltpu.CompilerParams(vmem_limit_bytes=VMEM),
        name="solve",
    )(factor, back, words, sh, sl)


def nt(a, b):
    return lax.dot_general(a, b, (((1,), (1,)), ((), ())), preferred_element_type=jnp.float32)


def nn(a, b):
    return jnp.dot(a, b, preferred_element_type=jnp.float32)


def encode_kernel(pieces, gram_ref, even_ref, *odd_refs):
    cycle = pl.program_id(0)
    half, width = gram_ref.shape[2], gram_ref.shape[5]
    codes = encode(gram_ref[:, 0, :, 0, 0, :].reshape(2 * half, width))
    even_ref[0] = codes[:half]
    for (start, count), odd_ref in zip(pieces, odd_refs):

        @pl.when((cycle >= start) & (cycle < start + count))
        def _(odd_ref=odd_ref):
            odd_ref[0] = codes[half:]


def encode_panel(gram, panel_width, pieces, after):
    _, _, half, col_cycles = gram.shape[:4]
    packed = panel_width // 2

    def piece_spec(start, count):
        return pl.BlockSpec((1, half, packed), lambda i: (jnp.clip(i - start, 0, count - 1), 0, 0))

    kernel = functools.partial(encode_kernel, pieces)
    return pl.pallas_call(
        lambda gram_ref, *refs: kernel(gram_ref, *refs[len(after) :]),
        out_shape=[jax.ShapeDtypeStruct((n, half, packed), jnp.int32) for n in [col_cycles] + [n for _, n in pieces]],
        grid=(col_cycles,),
        in_specs=[pl.BlockSpec((2, 1, half, 1, 1, panel_width), lambda i: (i, 0, 0, 0, 0, 0))]
        + [pl.BlockSpec(memory_space=pl.ANY)] * len(after),
        out_specs=[piece_spec(0, col_cycles)] + [piece_spec(*piece) for piece in pieces],
        compiler_params=pltpu.CompilerParams(vmem_limit_bytes=VMEM),
        cost_estimate=pl.CostEstimate(flops=1, bytes_accessed=1, transcendentals=0),
        name="encode_panel",
    )(gram, *after)


def encode_rows(gram, panel_width):
    cycles, _, half = gram.shape[:3]

    def kernel(gram_ref, out_ref):
        out_ref[0] = encode(gram_ref[0, 0, :, 0, 0, :])

    return pl.pallas_call(
        kernel,
        out_shape=jax.ShapeDtypeStruct((cycles, half, panel_width // 2), jnp.int32),
        grid=(cycles,),
        in_specs=[pl.BlockSpec((1, 1, half, 1, 1, panel_width), lambda i: (i, 0, 0, 0, 0, 0))],
        out_specs=pl.BlockSpec((1, half, panel_width // 2), lambda i: (i, 0, 0)),
        compiler_params=pltpu.CompilerParams(vmem_limit_bytes=VMEM),
        name="encode_rows",
    )(gram)


def small(kernel, shape, dtype, given, after, name, blocks=None):
    specs = [pl.BlockSpec(memory_space=pltpu.SMEM if x.ndim == 1 else pltpu.VMEM) for x in given]
    count = len(given)
    return pl.pallas_call(
        lambda *refs: kernel(*refs[:count], refs[-1]),
        out_shape=jax.ShapeDtypeStruct(shape, dtype),
        in_specs=specs + [pl.BlockSpec(memory_space=pl.ANY)] * len(after),
        out_specs=pl.BlockSpec(memory_space=pltpu.VMEM),
        compiler_params=pltpu.CompilerParams(vmem_limit_bytes=VMEM),
        cost_estimate=pl.CostEstimate(flops=1, bytes_accessed=1, transcendentals=0),
        name=name,
    )(*given, *after)


def choose(first, even, start, odd, after):
    count, half, packed = odd.shape

    def kernel(first_ref, even_ref, odd_ref, *refs):
        out_ref = refs[-1]

        @pl.when(first_ref[0] == 1)
        def _():
            out_ref[...] = even_ref[...]

        @pl.when(first_ref[0] == 0)
        def _():
            out_ref[...] = odd_ref[...]

    return pl.pallas_call(
        kernel,
        out_shape=jax.ShapeDtypeStruct(odd.shape, odd.dtype),
        grid=(count // 2,),
        in_specs=[
            pl.BlockSpec(memory_space=pltpu.SMEM),
            pl.BlockSpec((2, half, packed), lambda i: (start // 2 + i, 0, 0)),
            pl.BlockSpec((2, half, packed), lambda i: (i, 0, 0)),
        ]
        + [pl.BlockSpec(memory_space=pl.ANY)] * len(after),
        out_specs=pl.BlockSpec((2, half, packed), lambda i: (i, 0, 0)),
        compiler_params=pltpu.CompilerParams(vmem_limit_bytes=VMEM),
        cost_estimate=pl.CostEstimate(flops=1, bytes_accessed=1, transcendentals=0),
        name="choose",
    )(first, even, odd, *after)


def hold(x, after):
    return pl.pallas_call(
        lambda *refs: None,
        out_shape=jax.ShapeDtypeStruct(x.shape, x.dtype),
        in_specs=[pl.BlockSpec(memory_space=pl.ANY)] * (1 + len(after)),
        out_specs=pl.BlockSpec(memory_space=pl.ANY),
        input_output_aliases={0: 0},
        cost_estimate=pl.CostEstimate(flops=1, bytes_accessed=1, transcendentals=0),
        name="hold",
    )(x, *after)


def join(arrays, after):
    def kernel(*refs):
        for k, ref in enumerate(refs[:-1]):
            refs[-1][k] = ref[...]

    return small(kernel, (len(arrays),) + arrays[0].shape, arrays[0].dtype, arrays, after, "join")


def solve_kernel(pieces, factor_ref, back_ref, first_ref, own_even_ref, even_ref, sh_ref, sl_ref, *refs):
    odds, (high_ref, low_ref) = refs[: 2 * len(pieces)], refs[-2:]
    cycle = pl.program_id(0)
    half, packed = even_ref.shape[1:]

    def solved(words):
        total = None
        for part, values in enumerate(decode(words, factor_ref[0])):
            high, low = split(values)
            lines = pl.ds(part * packed, packed)
            one = nn(high, sh_ref[lines, :]) + nn(low, sh_ref[lines, :]) + nn(high, sl_ref[lines, :])
            total = one if total is None else total + one
        high_ref[...], low_ref[...] = split(total * back_ref[0])

    own = first_ref[0] == 1
    for p, (start, count) in enumerate(pieces):

        @pl.when((cycle * 2 >= start) & (cycle * 2 < start + count))
        def _(p=p):
            rows = []
            for i in range(2):
                rows.append(jnp.where(own, own_even_ref[i], even_ref[i]))
                rows.append(jnp.where(own, odds[2 * p][i], odds[2 * p + 1][i]))
            solved(jnp.concatenate(rows, axis=0))


def solve(factor, back, first, own_even, even, odds, pieces, sh, sl, after):
    col_cycles, half, packed = even.shape
    width = sh.shape[1]
    whole = pl.BlockSpec(sh.shape, lambda r: (0, 0))
    tile = pl.BlockSpec((4 * half, width), lambda r: (r, 0))
    scalars = pl.BlockSpec(memory_space=pltpu.SMEM)
    pair = pl.BlockSpec((2, half, packed), lambda r: (r, 0, 0))

    def piece_spec(start, count):
        return pl.BlockSpec((2, half, packed), lambda r: (jnp.clip(r - start // 2, 0, count // 2 - 1), 0, 0))

    return pl.pallas_call(
        functools.partial(solve_kernel, pieces),
        out_shape=[jax.ShapeDtypeStruct((2 * col_cycles * half, width), jnp.bfloat16)] * 2,
        grid=(col_cycles // 2,),
        in_specs=[scalars] * 3
        + [pair, pair, whole, whole]
        + [piece_spec(*piece) for piece in pieces for _ in range(2)]
        + [pl.BlockSpec(memory_space=pl.ANY)] * len(after),
        out_specs=[tile, tile],
        compiler_params=pltpu.CompilerParams(vmem_limit_bytes=VMEM),
        cost_estimate=pl.CostEstimate(flops=1, bytes_accessed=1, transcendentals=0),
        name="solve",
    )(factor, back, first, own_even, even, sh, sl, *[x for pair_of in odds for x in pair_of], *after)


def solve_rows(factor, back, words, sh, sl):
    rows, packed = words.shape
    width = sh.shape[1]
    step = min(rows, 256)

    def kernel(factor_ref, back_ref, words_ref, sh_ref, sl_ref, high_ref, low_ref):
        total = None
        for part, values in enumerate(decode(words_ref[...], factor_ref[0])):
            high, low = split(values)
            lines = pl.ds(part * packed, packed)
            one = nn(high, sh_ref[lines, :]) + nn(low, sh_ref[lines, :]) + nn(high, sl_ref[lines, :])
            total = one if total is None else total + one
        high_ref[...], low_ref[...] = split(total * back_ref[0])

    whole = pl.BlockSpec(sh.shape, lambda r: (0, 0))
    tile = pl.BlockSpec((step, width), lambda r: (r, 0))
    scalars = pl.BlockSpec(memory_space=pltpu.SMEM)
    return pl.pallas_call(
        kernel,
        out_shape=[jax.ShapeDtypeStruct((rows, width), jnp.bfloat16)] * 2,
        grid=(rows // step,),
        in_specs=[scalars, scalars, pl.BlockSpec((step, packed), lambda r: (r, 0)), whole, whole],
        out_specs=[tile, tile],
        compiler_params=pltpu.CompilerParams(vmem_limit_bytes=VMEM),
        name="solve_rows",
    )(factor, back, words, sh, sl)


def update_kernel(arrays, first_cycle, step, factor_ref, places_ref, high_ref, low_ref, *refs):
    words, refs = refs[:arrays], refs[arrays:]
    gram_ref, (out_ref, ph_ref, pl_ref, in_buf, out_buf, in_sem, out_sem) = refs[0], refs[-7:]
    cycle, tile, tiles = pl.program_id(0), pl.program_id(1), pl.num_programs(1)
    index, last = cycle * tiles + tile, pl.num_programs(0) * tiles - 1
    slot = lax.rem(index, 2)
    half, packed = words[0].shape[2:]

    def part(ref, at):
        return ref.at[pl.ds(lax.rem(at, tiles) * step, step), 0, :, at // tiles + first_cycle, 0, :]

    def load(at, side):
        return pltpu.make_async_copy(part(gram_ref, at), in_buf.at[side], in_sem.at[side])

    def store(at, side):
        return pltpu.make_async_copy(out_buf.at[side], part(out_ref, at), out_sem.at[side])

    @pl.when(index == 0)
    def _():
        load(0, 0).start()

    @pl.when(index < last)
    def _():
        load(index + 1, 1 - slot).start()

    @pl.when(tile == 0)
    def _():
        base = 0
        for words_ref in words:
            def member(k, carry, words_ref=words_ref, base=base):
                a, b = decode(words_ref[k, 0], factor_ref[0])
                ah, al = split(a)
                bh, bl = split(b)
                spot = pl.ds(pl.multiple_of(places_ref[base + k] * half, half), half)
                ph_ref[spot, :packed] = ah
                ph_ref[spot, packed:] = bh
                pl_ref[spot, :packed] = al
                pl_ref[spot, packed:] = bl
                return carry

            lax.fori_loop(0, words_ref.shape[0], member, 0)
            base += words_ref.shape[0]

    count = step * half
    spot = pl.ds(pl.multiple_of(tile * count, count), count)
    high, low = high_ref[spot, :], low_ref[spot, :]
    product = nt(high, ph_ref[...]) + nt(low, ph_ref[...]) + nt(high, pl_ref[...])
    load(index, slot).wait()

    @pl.when(index >= 2)
    def _():
        store(index - 2, slot).wait()

    out_buf[slot] = in_buf[slot] - product.reshape(step, half, out_buf.shape[3])
    store(index, slot).start()

    @pl.when(index == last)
    def _():
        @pl.when(index >= 1)
        def _():
            store(index - 1, 1 - slot).wait()

        store(index, slot).wait()


def update(gram, before, factor, places, high, low, words, begin, count, first_cycle, after):
    cycles, _, half, _, _, block = gram.shape
    packed = words[0].shape[3]
    step = max(1, 512 // half)
    scalars, anywhere = pl.BlockSpec(memory_space=pltpu.SMEM), pl.BlockSpec(memory_space=pl.ANY)
    given = [factor, places, high, low, *words, gram]
    specs = [scalars, scalars] + [pl.BlockSpec(high.shape, lambda c, r: (0, 0))] * 2
    specs += [pl.BlockSpec((w.shape[0], 1, half, packed), lambda c, r: (0, c + begin, 0, 0)) for w in words]
    specs.append(anywhere)
    aliases = {}
    if before is not None:
        aliases = {len(given): 0}
        given.append(before)
        specs.append(anywhere)
    given += after
    specs += [anywhere] * len(after)
    return pl.pallas_call(
        functools.partial(update_kernel, len(words), first_cycle, step),
        out_shape=jax.ShapeDtypeStruct(gram.shape, gram.dtype),
        grid=(count, cycles // step),
        in_specs=specs,
        out_specs=anywhere,
        scratch_shapes=[pltpu.VMEM((block, 2 * packed), jnp.bfloat16)] * 2
        + [pltpu.VMEM((2, step, half, block), jnp.float32)] * 2
        + [pltpu.SemaphoreType.DMA((2,))] * 2,
        input_output_aliases=aliases,
        compiler_params=pltpu.CompilerParams(vmem_limit_bytes=VMEM),
        cost_estimate=pl.CostEstimate(flops=8 * cycles * half * count * block * 2 * packed, bytes_accessed=1, transcendentals=0),
        name="trailing_update",
    )(*given)


def gather_blocks(parts, places_ref, whole_ref):
    base = 0
    for part_ref in parts:
        size = part_ref.shape[1]

        def member(k, carry, part_ref=part_ref, base=base, size=size):
            spot = pl.ds(pl.multiple_of(places_ref[base + k] * size, size), size)
            whole_ref[spot, :] = part_ref[k]
            return carry

        lax.fori_loop(0, part_ref.shape[0], member, 0)
        base += part_ref.shape[0]


def residual_kernel(arrays, back_ref, places_ref, high_ref, low_ref, cross_ref, *refs):
    parts, (dh_ref, dl_ref, lead_ref) = refs[:arrays], refs[-3:]
    rows, half, count = cross_ref.shape[0], cross_ref.shape[2], cross_ref.shape[3]
    pl.when(pl.program_id(0) == 0)(lambda: gather_blocks(parts, places_ref, lead_ref))
    lead = lead_ref[: high_ref.shape[1], :]
    removed = nn(high_ref[...], lead) + nn(low_ref[...], lead)
    cross = cross_ref[:, 0].reshape(rows * half, count).astype(jnp.float32)
    dh_ref[...], dl_ref[...] = split(cross - removed * back_ref[0])


def residual(back, places, high, low, cross, parts, after):
    cycles, _, half, count = cross.shape
    step = max(1, 256 // half)
    panel = high.shape[1]
    scalars = pl.BlockSpec(memory_space=pltpu.SMEM)
    whole = lambda part: pl.BlockSpec(part.shape, lambda r: (0, 0, 0))
    tile = pl.BlockSpec((step * half, panel), lambda r: (r, 0))
    out = pl.BlockSpec((step * half, count), lambda r: (r, 0))
    total = sum(part.shape[0] for part in parts) * parts[0].shape[1]
    return pl.pallas_call(
        functools.partial(residual_kernel, len(parts)),
        out_shape=[jax.ShapeDtypeStruct((cycles * half, count), jnp.bfloat16)] * 2,
        grid=(cycles // step,),
        in_specs=[scalars, scalars, tile, tile, pl.BlockSpec((step, 1, half, count), lambda r: (r, 0, 0, 0))]
        + [whole(part) for part in parts]
        + [pl.BlockSpec(memory_space=pl.ANY)] * len(after),
        out_specs=[out, out],
        scratch_shapes=[pltpu.VMEM((total, count), jnp.bfloat16)],
        compiler_params=pltpu.CompilerParams(vmem_limit_bytes=VMEM),
        cost_estimate=pl.CostEstimate(flops=9 * 10**9, bytes_accessed=1, transcendentals=0),
        name="residual",
    )(back, places, high, low, cross, *parts, *after)


def rhs_kernel(arrays, places_ref, dh_ref, dl_ref, *refs):
    parts, (out_ref, lost_ref) = refs[:arrays], refs[-2:]
    pl.when(pl.program_id(0) == 0)(lambda: gather_blocks(parts, places_ref, lost_ref))
    out = nn(dh_ref[...], lost_ref[...]) + nn(dl_ref[...], lost_ref[...])
    out_ref[:, 0] = out.reshape(out_ref.shape[0], out_ref.shape[2], out.shape[1])


def rhs_step(places, dh, dl, cycles, parts, after):
    count = dh.shape[1]
    half = dh.shape[0] // cycles
    width = parts[0].shape[2]
    step = max(1, 256 // half)
    whole = lambda part: pl.BlockSpec(part.shape, lambda r: (0, 0, 0))
    tile = pl.BlockSpec((step * half, count), lambda r: (r, 0))
    return pl.pallas_call(
        functools.partial(rhs_kernel, len(parts)),
        out_shape=jax.ShapeDtypeStruct((cycles, 1, half, width), jnp.float32),
        grid=(cycles // step,),
        in_specs=[pl.BlockSpec(memory_space=pltpu.SMEM), tile, tile]
        + [whole(part) for part in parts]
        + [pl.BlockSpec(memory_space=pl.ANY)] * len(after),
        out_specs=pl.BlockSpec((step, 1, half, width), lambda r: (r, 0, 0, 0)),
        scratch_shapes=[pltpu.VMEM((count, width), jnp.bfloat16)],
        compiler_params=pltpu.CompilerParams(vmem_limit_bytes=VMEM),
        cost_estimate=pl.CostEstimate(flops=14 * 10**9, bytes_accessed=1, transcendentals=0),
        name="rhs_step",
    )(places, dh, dl, *parts, *after)


def square_kernel(turned_ref, *refs):
    high_ref, low_ref = refs[-2:]
    high_ref[...], low_ref[...] = split(nt(turned_ref[...], turned_ref[...]))


def square(turned, after):
    whole = pl.BlockSpec(memory_space=pltpu.VMEM)
    return pl.pallas_call(
        square_kernel,
        out_shape=[jax.ShapeDtypeStruct(turned.shape, jnp.bfloat16)] * 2,
        in_specs=[whole] + [pl.BlockSpec(memory_space=pl.ANY)] * len(after),
        out_specs=[whole] * 2,
        compiler_params=pltpu.CompilerParams(vmem_limit_bytes=VMEM),
        cost_estimate=pl.CostEstimate(flops=1, bytes_accessed=1, transcendentals=0),
        name="square",
    )(turned, *after)


def own_kernel(order_ref, range_ref, places_ref, rows_ref, *refs):
    out_ref = refs[-1]
    count = out_ref.shape[0]
    start = order_ref[pl.program_id(0)] * count
    any_own = (range_ref[0] < start + count) & (range_ref[1] > start)

    @pl.when(any_own)
    def _():
        shard = rows_ref.shape[0]
        lines = lax.broadcasted_iota(jnp.int32, (count, shard), 1)
        picks = jnp.where(places_ref[...] == lines, 1.0, 0.0).astype(jnp.bfloat16)
        out_ref[...] = nn(picks, rows_ref[...]).astype(jnp.bfloat16)

    @pl.when(jnp.logical_not(any_own))
    def _():
        out_ref[...] = jnp.zeros_like(out_ref)


def own_lost_rows(down_rows, places, span, order, size, after):
    shard, width = down_rows.shape
    return pl.pallas_call(
        own_kernel,
        grid_spec=pltpu.PrefetchScalarGridSpec(
            num_scalar_prefetch=2,
            grid=(order.shape[0],),
            in_specs=[
                pl.BlockSpec((size, 1), lambda i, order, span: (order[i], 0)),
                pl.BlockSpec(down_rows.shape, lambda i, order, span: (0, 0)),
                *[pl.BlockSpec(memory_space=pl.ANY)] * len(after),
            ],
            out_specs=pl.BlockSpec((size, width), lambda i, order, span: (i, 0)),
        ),
        out_shape=jax.ShapeDtypeStruct((order.shape[0] * size, width), jnp.bfloat16),
        compiler_params=pltpu.CompilerParams(vmem_limit_bytes=VMEM),
        cost_estimate=pl.CostEstimate(flops=1, bytes_accessed=1, transcendentals=0),
        name="own_lost_rows",
    )(order, span, places, down_rows, *after)


def turn(x, k):
    far = lax.axis_size("far")
    return lax.ppermute(x, "far", [(r, (r + k) % far) for r in range(far)])


def near(x):
    return lax.ppermute(x, "near", [(0, 1), (1, 0)])


def other(x):
    return lax.ppermute(x, "tp", [(0, 1), (1, 0)])


def far_order():
    far = lax.axis_size("far")
    return sorted(range(1, far), key=lambda k: min(k, far - k))


def member_at(place, flips):
    return (place * 2 + (lax.axis_index("near") ^ flips[0])) * 2 + (lax.axis_index("tp") ^ flips[1])


def spread(line, after):
    plane = [line, near(line)]
    if after:
        plane[1] = hold(plane[1], after)
    return plane + [other(x) for x in plane]


def add(a, b, after):
    def kernel(a_ref, b_ref, out_ref):
        out_ref[...] = a_ref[...] + b_ref[...]

    return small(kernel, a.shape, a.dtype, [a, b], after, "add")


def add_halves(a, b, after):
    count = a.shape[0] // 2

    def kernel(a_ref, b_ref, *refs):
        refs[-2][...] = a_ref[:count] + b_ref[:count]
        refs[-1][...] = a_ref[count:] + b_ref[count:]

    whole = pl.BlockSpec(memory_space=pltpu.VMEM)
    return pl.pallas_call(
        kernel,
        out_shape=[jax.ShapeDtypeStruct((count, a.shape[1]), a.dtype)] * 2,
        in_specs=[whole] * 2 + [pl.BlockSpec(memory_space=pl.ANY)] * len(after),
        out_specs=[whole] * 2,
        compiler_params=pltpu.CompilerParams(vmem_limit_bytes=VMEM),
        cost_estimate=pl.CostEstimate(flops=1, bytes_accessed=1, transcendentals=0),
        name="add_halves",
    )(a, b, *after)


def table(members):
    return jnp.stack(members).astype(jnp.int32)


def per_device(gram, inv_factor, cross_gram, down_rows, removed):
    cycles, _, half, col_cycles, _, block = gram.shape
    panel_width = inv_factor.shape[0]
    packed = panel_width // 2
    cols, count = lax.axis_size("col"), removed.shape[0]
    far, order = lax.axis_size("far"), far_order()
    members = lax.axis_size(MEMBERS)
    first = (lax.axis_index("col") == 0).astype(jnp.int32).reshape(1)
    here = lax.axis_index("far")
    flips = [(n, t) for t in (0, 1) for n in (0, 1)]
    around = table([member_at((here - k) % far, flip) for flip in flips for k in [0] + order])
    lined = table([member_at(z, flip) for flip in flips for z in range(far)])
    unit = LIMIT / LEVELS**2

    lead_turns = [turn(cross_gram[0, 0], k) for k in order]

    largest = jnp.max(jnp.abs(inv_factor)).astype(jnp.float32)
    scale = jnp.where(largest > 2.0**40, 2.0**-80, jnp.where(largest < 2.0**-40, 2.0**80, 1.0))
    back = jnp.where(largest > 2.0**40, 2.0**80, jnp.where(largest < 2.0**-40, 2.0**-80, 1.0)).reshape(1)
    turned = (inv_factor.astype(jnp.float32) * scale).astype(jnp.bfloat16).T
    units = jnp.full((1,), unit, jnp.float32)

    size = count // members
    places = (removed - lax.axis_index(MEMBERS) * down_rows.shape[0]).reshape(count, 1)
    span = jnp.stack([jnp.sum(places < 0), jnp.sum(places < down_rows.shape[0])]).astype(jnp.int32)
    blocks = [table([member_at(z, (n, t)) for n in (0, 1) for z in range(far)]) for t in (0, 1)]

    if cols == 2 and col_cycles == 8:
        cuts = PIECES
        even, *odds = encode_panel(gram, panel_width, cuts, [])
        to_one = lambda x: lax.ppermute(x, "col", [(0, 1)])
        got_odds = [to_one(x) for x in odds]
        last = even
    else:
        cuts = ((0, col_cycles),)
        by_cycle = encode_rows(gram, panel_width).reshape(col_cycles, cols, half, packed)
        sent = sum(lax.ppermute(by_cycle, "col", [(0, c)]) for c in range(1, cols))
        mine = jnp.where(first[0] == 1, by_cycle, sent)
        wanted = [lax.dynamic_index_in_dim(mine, lax.axis_index("col"), axis=1, keepdims=False)]
        last = by_cycle
    give = last = own_lost_rows(down_rows, places, span, blocks[1], size, [last])
    got = other(give)
    split_panel = cols == 2 and col_cycles == 8
    gathered = []

    def gather(piece):
        return lax.all_gather(piece, "far", axis=0, tiled=False)

    if split_panel:
        last = wanted = choose(first, even, cuts[0][0], got_odds[0], [last])
        gathered.append(gather(wanted))
    else:
        gathered.append(gather(wanted[0]))
    keep = last = own_lost_rows(down_rows, places, span, blocks[0], size, [last])
    if split_panel:
        for (start, _), got_odd in list(zip(cuts, got_odds))[1:]:
            last = wanted = choose(first, even, start, got_odd, [last])
            gathered.append(gather(wanted))
        got_even = to_one(hold(even, [last]))
    kept, given = add_halves(keep, got, [last])
    near_got, last = near(given), given
    if split_panel:
        sh, sl = square(turned, [last, got_even, near_got])
        high, low = solve(units, back, first, even, got_even, list(zip(odds, got_odds)), cuts, sh, sl, [])
    else:
        sh, sl = square(turned, [last])
        high, low = solve_rows(units, back, mine.reshape(cycles * half, packed), sh, sl)
    if split_panel:
        gathered[0] = hold(gathered[0], [near_got, got_even])
    lead_line = join([cross_gram[0, 0]] + lead_turns, [high])
    lead_parts = spread(lead_line, [])
    kept = add(kept, near_got, [lead_line, *gathered[1:]])
    w_own = lax.psum_scatter(kept, "far", scatter_dimension=0, tiled=True)


    dh, dl = residual(back, around, high, low, cross_gram, lead_parts, [kept])
    updated, index = None, 0
    for line, (start, n) in zip(gathered, cuts):
        arrays = spread(line, [kept if updated is None else updated])
        part = STEP if n % STEP == 0 else n
        for begin in range(0, n, part):
            after = [dh] if index == 0 else []
            updated = update(gram, updated, units * back, lined, high, low, arrays, begin, part, start + begin, after)
            if index == 0:
                w_line = lax.all_gather(hold(w_own, [updated]), "far", axis=0, tiled=False)
            if index == 2:
                w_line = hold(w_line, [updated])
            if index == 3 or n == part:
                w_parts = spread(w_line, [updated])
            index += 1
    rhs_next = rhs_step(lined, dh, dl, cycles, w_parts, [updated])
    return updated, rhs_next


def solution(mesh):
    rows, cols, tps = (mesh.shape[axis] for axis in ("row", "col", "tp"))
    cut = jax.sharding.Mesh(mesh.devices.reshape(rows // 2, 2, cols, tps), ("far", "near", "col", "tp"))
    row = ("far", "near")
    return jax.shard_map(
        per_device,
        mesh=cut,
        in_specs=(
            P(None, row, "tp", None, "col", None),
            P(),
            P(None, row, "tp", None),
            P((*row, "tp"), "col"),
            P(),
        ),
        out_specs=(P(None, row, "tp", None, "col", None), P(None, row, "tp", "col")),
        check_vma=False,
    )
```

time: 586 us -> 291 us (0.50); the launches traced: 577 us -> 288 us
  waiting for transfers between devices: 265 us -> 59.5 us
  matrix products: 187 us -> 0 us
  Pallas kernels: 0 us -> 165 us
  local copies, waits for them, and re-layouts: 99.5 us -> 16.3 us
  starting transfers between devices: 0.38 us -> 25.3 us
    all_gather x3, waiting for transfers between devices: 265 us -> 13.8 us  [the longest x2 13.8 us: gather(): return lax.all_gather(piece, 'far', axis=0, tiled=False)]
    dot_general x5 -> x0, matrix products: 187 us -> none  [the longest x1 113 us: per_device(): jnp.einsum('rp,cwp->rcw', left, lax.all_gather(wanted, ('row', 'tp'), axi...]
    pallas_call x0 -> x23, Pallas kernels: none -> 165 us  [the longest x4 87.3 us: update(): pl.pallas_call(functools.partial(update_kernel, len(words), first_cycle,...]
    unnamed x15 -> x38, local copies, waits for them, and re-layouts: 73.5 us -> 11.7 us
    ppermute x0 -> x20, waiting for transfers between devices: none -> 45.6 us  [the longest x5 21.4 us: near(): return lax.ppermute(x, 'near', [(0, 1), (1, 0)])]
    gather x3 -> x0, local copies, waits for them, and re-layouts: 25.2 us -> none  [the longest x1 16.7 us: per_device(): lost_rows = jnp.take(everyone, owner * capacity + within, axis=0)]
    ppermute x0 -> x20, starting transfers between devices: none -> 25 us  [the longest x3 12.8 us: per_device(): to_one = lambda x: lax.ppermute(x, 'col', [(0, 1)])]
    select_n x4 -> x0, other arithmetic: 6.81 us -> none  [the longest x1 5.02 us: broadcast(): jnp.where(lax.axis_index(axis) == holder, block, jnp.zeros_like(block))]
  transfers between devices with their start and end apart: 4 -> 24, of which waited for: 3 -> 7; matrix products, arithmetic and copies ran while one was open for 22% -> 6% of each run, Pallas kernels for 0% -> 49%
where the time goes in v1:
time: 291 us; the launch traced here: 288 us
  Pallas kernels  165 us (57%)
  waiting for transfers between devices  59.5 us (20%)
  starting transfers between devices  25.3 us (9%)
  local copies, waits for them, and re-layouts  16.3 us (6%)
  between operations  15.4 us (5%)
  other arithmetic  6.98 us (2%)
    pallas_call x4, Pallas kernels, update(): pl.pallas_call(functools.partial(update_kernel, len(words), first_cycle,...  87.3 us
    ppermute x5, waiting for transfers between devices, near(): return lax.ppermute(x, 'near', [(0, 1), (1, 0)])  21.4 us
    pallas_call x2, Pallas kernels, own_lost_rows(): pl.pallas_call(own_kernel, grid_spec=pltpu.PrefetchScalarGridSpec(num_sca...  17.4 us
    ppermute x3, waiting for transfers between devices, per_device(): to_one = lambda x: lax.ppermute(x, 'col', [(0, 1)])  17.3 us
    all_gather x2, waiting for transfers between devices, gather(): return lax.all_gather(piece, 'far', axis=0, tiled=False)  13.8 us
    pallas_call x1, Pallas kernels, rhs_step(): pl.pallas_call(functools.partial(rhs_kernel, len(parts)), out_shape=jax.S...  13.6 us
    ppermute x3, starting transfers between devices, per_device(): to_one = lambda x: lax.ppermute(x, 'col', [(0, 1)])  12.8 us
    unnamed x38, local copies, waits for them, and re-layouts  11.7 us
  transfers between devices with their start and end apart: 24, of which 7 were waited for; matrix products, arithmetic and copies ran while one was open for 6% of the time, Pallas kernels for 49%

profile of v1, /device:TPU:0, one launch (start us, length us, event | category | flops | bytes accessed | tf_op | source)
XLA Modules:
  0.0 288.3 jit_solution(2649778736903749450)
XLA Ops:
  7.2 7.5 %encode_panel.1 = (s32[8,64,512]{2,1,0:T(8,128)}, s32[4,64,512]{2,1,0:T(8,128)}, s32[4,64,512]{2,1,0:T(8,128)}) custom-call(f32[16,1,64,8,1,1024]{5,4,3,2,1,0:T(1,128)} %refs_4_.7), custom_call_target="tpu_custom_call" | custom-call | flops 1 | bytes 1 | tf_op jit(solution)/shard_map/encode_panel/pallas_call | solution.py:115
  14.7 4.9 %collective-permute-start.1 = (s32[4,64,512]{2,1,0:T(8,128)}, s32[4,64,512]{2,1,0:T(8,128)S(1)}, u32[]{:S(2)}, u32[]{:S(2)}) collective-permute-start(s32[4,64,512]{2,1,0:T(8,128)} %get-tuple-element.15.refs_0_), channel_id=1, source_target_pairs={{0,2},{1,3},{4,6},{5,7},{8,10},{9,11},{12,14},{13,15},{16,18},{17,... | collective-permute-start | bytes 1572872 | tf_op jit(solution)/shard_map/ppermute | solution.py:610
  20.3 1.0 copy.22.places_ref
  22.0 1.9 pad_add_fusion.range_ref
  23.9 7.8 %own_lost_rows.2.refs_0_ = bf16[512,2048]{1,0:T(8,128)(2,1)} custom-call(s32[8]{0:T(128)} %stack.154.order_ref, s32[2]{0:T(128)} %pad_add_fusion.range_ref, s32[1024,1]{1,0:T(8,128)} %copy.22.places_ref, bf16[1848,2048]{1,0:T(8,128)(2,1)} %rows_ref.3, s32[8,64,512]{2,1,0:T(8,128)} %get-tuple-element.13.refs_0_.even_ref.own_even_ref), custom_call_target="tpu_custom_call" | custom-call | flops 1 | bytes 1 | tf_op jit(solution)/shard_map/own_lost_rows/pallas_call | solution.py:502
  31.6 0.8 copy-done.7
  32.5 2.1 choose.2.refs_0_
  34.6 1.1 collective-permute-start.3
  35.7 3.5 %collective-permute-start = (s32[4,64,512]{2,1,0:T(8,128)}, s32[4,64,512]{2,1,0:T(8,128)}, u32[]{:S(2)}, u32[]{:S(2)}) collective-permute-start(s32[4,64,512]{2,1,0:T(8,128)} %get-tuple-element.14.refs_2_), channel_id=1, source_target_pairs={{0,2},{1,3},{4,6},{5,7},{8,10},{9,11},{12,14},{13,15},{16,18},{17,... | collective-permute-start | bytes 1572872 | tf_op jit(solution)/shard_map/ppermute | solution.py:610
  39.2 0.7 stack.150.order_ref
  39.9 1.0 copy.24.refs_0_
  40.9 9.6 %own_lost_rows.3.refs_0_.a_ref = bf16[512,2048]{1,0:T(8,128)(2,1)} custom-call(s32[8]{0:T(128)} %stack.150.order_ref, s32[2]{0:T(128)} %pad_add_fusion.range_ref, s32[1024,1]{1,0:T(8,128)} %copy.22.places_ref, bf16[1848,2048]{1,0:T(8,128)(2,1)} %rows_ref.3, s32[4,64,512]{2,1,0:T(8,128)} %choose.2.refs_0_), custom_call_target="tpu_custom_call" | custom-call | flops 1 | bytes 1 | tf_op jit(solution)/shard_map/own_lost_rows/pallas_call | solution.py:502
  50.5 1.9 choose.3.refs_1_.refs_0_
  52.5 4.4 %collective-permute-start.2 = (s32[8,64,512]{2,1,0:T(8,128)}, s32[8,64,512]{2,1,0:T(8,128)S(1)}, u32[]{:S(2)}, u32[]{:S(2)}) collective-permute-start(s32[8,64,512]{2,1,0:T(8,128)} %hold.7), channel_id=1, source_target_pairs={{0,2},{1,3},{4,6},{5,7},{8,10},{9,11},{12,14},{13,15},{16,18},{17,... | collective-permute-start | bytes 3145736 | tf_op jit(solution)/shard_map/ppermute | solution.py:610
  57.0 3.7 %add_halves.1 = (bf16[256,2048]{1,0:T(8,128)(2,1)}, bf16[256,2048]{1,0:T(8,128)(2,1)}) custom-call(bf16[512,2048]{1,0:T(8,128)(2,1)} %own_lost_rows.3.refs_0_.a_ref, bf16[512,2048]{1,0:T(8,128)(2,1)} %collective-permute-done.3.b_ref, s32[4,64,512]{2,1,0:T(8,128)} %choose.3.refs_1_.refs_0_), custom_call_target="tpu_custom_call" | custom-call | flops 1 | bytes 1 | tf_op jit(solution)/shard_map/add_halves/pallas_call | solution.py:565
  60.7 1.5 collective-permute-start.4
  62.2 17.3 %collective-permute-done.2.refs_1_.even_ref.refs_2_ = s32[8,64,512]{2,1,0:T(8,128)S(1)} collective-permute-done((s32[8,64,512]{2,1,0:T(8,128)}, s32[8,64,512]{2,1,0:T(8,128)S(1)}, u32[]{:S(2)}, u32[]{:S(2)}) %collective-permute-start.2) | collective-permute-done | bytes 1048608 | tf_op jit(solution)/shard_map/ppermute | solution.py:610
  79.5 5.9 %collective-permute-done.4.refs_2_.refs_1_ = bf16[256,2048]{1,0:T(8,128)(2,1)S(1)} collective-permute-done((bf16[256,2048]{1,0:T(8,128)(2,1)}, bf16[256,2048]{1,0:T(8,128)(2,1)S(1)}, u32[]{:S(2)}, u32[]{:S(2)}) %collective-permute-start.4) | collective-permute-done | bytes 1048608 | tf_op jit(solution)/shard_map/ppermute | solution.py:527
  85.4 1.0 copy-done.3
  86.4 1.5 collective-permute-start.6
  87.9 0.9 slice_bitcast_fusion.refs_0_
  88.8 1.6 collective-permute-start.7
  90.4 2.3 collective-permute-start.8
  92.7 0.7 collective-permute-start.9
  93.5 3.9 %copy.23 = bf16[1024,1024]{0,1:T(8,128)(2,1)} copy(bf16[1024,1024]{1,0:T(8,128)(2,1)} %param.6) | data formatting | bytes 4194304 | tf_op args[1]
  97.4 1.0 abs_reduce_fusion
  99.7 3.4 %fusion.turned_ref = bf16[1024,1024]{1,0:T(8,128)(2,1)} fusion(bf16[1024,1024]{0,1:T(8,128)(2,1)} %copy.23, f32[]{:T(128)S(6)} %select_n.60), kind=kLoop, calls=%fused_computation.1 | loop fusion | flops 3145728 | bytes 4194308 | tf_op jit(solution)/shard_map/transpose | solution.py:599
  103.2 6.0 %square.1 = (bf16[1024,1024]{1,0:T(8,128)(2,1)}, bf16[1024,1024]{1,0:T(8,128)(2,1)}) custom-call(bf16[1024,1024]{1,0:T(8,128)(2,1)} %fusion.turned_ref, bf16[256,2048]{1,0:T(8,128)(2,1)} %get-tuple-element.16.refs_0_, s32[8,64,512]{2,1,0:T(8,128)} %copy-done.2, bf16[256,2048]{1,0:T(8,128)(2,1)} %copy-done.3), custom_call_target="tpu_custom_call" | custom-call | flops 1 | bytes 1 | tf_op jit(solution)/shard_map/square/pallas_call | solution.py:471
  109.1 11.5 %solve.1 = (bf16[1024,1024]{1,0:T(8,128)(2,1)}, bf16[1024,1024]{1,0:T(8,128)(2,1)}) custom-call(f32[1]{0:T(128)} %constant.81.clone.1.factor_ref, f32[1]{0:T(128)} %bitcast.back_ref, s32[1]{0:T(128)} %bitcast.17.first_ref, s32[8,64,512]{2,1,0:T(8,128)} %get-tuple-element.13.refs_0_.even_ref.own_even_ref, s32[8,64,512]{2,1,0:T(8,128)} %copy-done.2, ...), custom_call_target="tpu_custom_call" | custom-call | flops 1 | bytes 1 | tf_op jit(solution)/shard_map/solve/pallas_call | solution.py:247
  121.4 2.0 join.1.refs_2_.refs_0_
  123.4 13.8 %all-gather.7.cloned.1.call-done = s32[16,64,512]{2,1,0:T(8,128)} async-done(((s32[4,64,512]{2,1,0:T(8,128)}), s32[16,64,512]{2,1,0:T(8,128)}) %all-gather.7.cloned.1.call-update) | async-done | bytes 2097168 | tf_op jit(solution)/shard_map/all_gather | solution.py:626
  137.1 2.6 add.269.refs_1_.refs_4_
  139.9 1.0 copy-done.8
  141.3 13.4 %collective-permute-done.12.refs_1_ = bf16[4,64,1024]{2,1,0:T(8,128)(2,1)S(1)} collective-permute-done((bf16[4,64,1024]{2,1,0:T(8,128)(2,1)S(1)}, bf16[4,64,1024]{2,1,0:T(8,128)(2,1)S(1)}, u32[]{:S(2)}, u32[]{:S(2)}) %collective-permute-start.12) | collective-permute-done | bytes 524320 | tf_op jit(solution)/shard_map/ppermute | solution.py:527
  154.7 0.7 stack.149.places_ref
  157.0 9.2 %residual.1 = (bf16[1024,1024]{1,0:T(8,128)(2,1)}, bf16[1024,1024]{1,0:T(8,128)(2,1)}) custom-call(f32[1]{0:T(128)} %bitcast.back_ref, s32[16]{0:T(128)} %stack.171.places_ref, bf16[1024,1024]{1,0:T(8,128)(2,1)} %get-tuple-element.19.refs_4_.high_ref, bf16[1024,1024]{1,0:T(8,128)(2,1)} %get-tuple-element.20.low_ref, bf16[16,1,64,1024]{3,2,1,0:T(8,128)(2,1)} %cross_ref.1, ...), custom_call_target="tpu_custom_call" | custom-call | flops 8999999488 | bytes 1 | tf_op jit(solution)/shard_map/residual/pallas_call | solution.py:420
  166.3 21.8 %trailing_update.4.refs_5_.refs_1_ = f32[16,1,64,8,1,1024]{5,4,3,2,1,0:T(1,128)} custom-call(f32[1]{0:T(128)S(6)} %mul_broadcast_in_dim.2.factor_ref, s32[16]{0:T(128)} %stack.149.places_ref, bf16[1024,1024]{1,0:T(8,128)(2,1)} %get-tuple-element.19.refs_4_.high_ref, bf16[1024,1024]{1,0:T(8,128)(2,1)} %get-tuple-element.20.low_ref, ...), custom_call_target="tpu_custom_call" | custom-call | flops 17179869184 | bytes 1 | tf_op jit(solution)/shard_map/trailing_update/pallas_call | solution.py:371
  188.1 21.8 %trailing_update.5.refs_1_.refs_5_ = f32[16,1,64,8,1,1024]{5,4,3,2,1,0:T(1,128)} custom-call(f32[1]{0:T(128)S(6)} %mul_broadcast_in_dim.2.factor_ref, s32[16]{0:T(128)} %stack.149.places_ref, bf16[1024,1024]{1,0:T(8,128)(2,1)} %get-tuple-element.19.refs_4_.high_ref, bf16[1024,1024]{1,0:T(8,128)(2,1)} %get-tuple-element.20.low_ref, ...), custom_call_target="tpu_custom_call", output_to_operand_aliasing={{}: (9, {})} | custom-call | flops 17179869184 | bytes 1 | tf_op jit(solution)/shard_map/trailing_update/pallas_call | solution.py:371
  210.4 4.0 %collective-permute-done.16.refs_3_ = s32[4,4,64,512]{3,2,1,0:T(8,128)S(1)} collective-permute-done((s32[4,4,64,512]{3,2,1,0:T(8,128)}, s32[4,4,64,512]{3,2,1,0:T(8,128)S(1)}, u32[]{:S(2)}, u32[]{:S(2)}) %collective-permute-start.16) | collective-permute-done | bytes 2097184 | tf_op jit(solution)/shard_map/ppermute | solution.py:531
  214.3 1.3 copy-done.4
  215.6 21.9 %trailing_update.6.refs_5_.refs_1_ = f32[16,1,64,8,1,1024]{5,4,3,2,1,0:T(1,128)} custom-call(f32[1]{0:T(128)S(6)} %mul_broadcast_in_dim.2.factor_ref, s32[16]{0:T(128)} %stack.149.places_ref, bf16[1024,1024]{1,0:T(8,128)(2,1)} %get-tuple-element.19.refs_4_.high_ref, bf16[1024,1024]{1,0:T(8,128)(2,1)} %get-tuple-element.20.low_ref, ...), custom_call_target="tpu_custom_call", output_to_operand_aliasing={{}: (9, {})} | custom-call | flops 17179869184 | bytes 1 | tf_op jit(solution)/shard_map/trailing_update/pallas_call | solution.py:371
  237.6 1.6 collective-permute-start.17
  239.3 21.9 %trailing_update.7.refs_1_.refs_4_ = f32[16,1,64,8,1,1024]{5,4,3,2,1,0:T(1,128)} custom-call(f32[1]{0:T(128)S(6)} %mul_broadcast_in_dim.2.factor_ref, s32[16]{0:T(128)} %stack.149.places_ref, bf16[1024,1024]{1,0:T(8,128)(2,1)} %get-tuple-element.19.refs_4_.high_ref, bf16[1024,1024]{1,0:T(8,128)(2,1)} %get-tuple-element.20.low_ref, ...), custom_call_target="tpu_custom_call", output_to_operand_aliasing={{}: (9, {})} | custom-call | flops 17179869184 | bytes 1 | tf_op jit(solution)/shard_map/trailing_update/pallas_call | solution.py:371
  261.2 2.1 collective-permute-done.17.refs_0_
  263.3 1.0 copy-done.9
  264.3 2.9 collective-permute-done.19.refs_3_
  267.1 1.0 copy-done.16
  268.1 13.6 %rhs_step.1 = f32[16,1,64,2048]{3,2,1,0:T(8,128)} custom-call(s32[16]{0:T(128)} %stack.149.places_ref, bf16[1024,1024]{1,0:T(8,128)(2,1)} %get-tuple-element.22.refs_5_.dh_ref, bf16[1024,1024]{1,0:T(8,128)(2,1)} %get-tuple-element.23.dl_ref, bf16[4,64,2048]{2,1,0:T(8,128)(2,1)} %hold.12.refs_0_, bf16[4,64,2048]{2,1,0:T(8,128)(2,1)} %hold.13.refs_1_, ...), custom_call_target="tpu_custom_call" | custom-call | flops 14000000000 | bytes 1 | tf_op jit(solution)/shard_map/rhs_step/pallas_call | solution.py:449
  (75 shorter events, 5.0 us)
Async XLA Ops:
  7.2 12.5 %copy-start.14 = (s32[1024]{0:T(1024)S(1)}, s32[1024]{0:T(1024)}, u32[]{:S(2)}) copy-start(s32[1024]{0:T(1024)} %param.9) | copy-start | bytes 12292
  7.2 78.2 %all-gather.9.cloned.1.call-start = ((), (), s32[]{:S(2)}) async-start(), calls=%async_computation.3 | async-start | bytes 2621440 | tf_op jit(solution)/shard_map/all_gather | solution.py:626
  14.7 16.9 %collective-permute-start.1 = (s32[4,64,512]{2,1,0:T(8,128)}, s32[4,64,512]{2,1,0:T(8,128)S(1)}, u32[]{:S(2)}, u32[]{:S(2)}) collective-permute-start(s32[4,64,512]{2,1,0:T(8,128)} %get-tuple-element.15.refs_0_), channel_id=1, source_target_pairs={{0,2},{1,3},{4,6},{5,7},{8,10},{9,11},{12,14},{13,15},{16,18},{17,... | collective-permute-start | bytes 1572872 | tf_op jit(solution)/shard_map/ppermute | solution.py:610
  31.6 0.8 copy-start.7
  32.5 2.2 copy-start.6
  32.5 7.4 %copy-start = (s32[8,64,512]{2,1,0:T(8,128)S(1)}, s32[8,64,512]{2,1,0:T(8,128)}, u32[]{:S(2)}) copy-start(s32[8,64,512]{2,1,0:T(8,128)} %get-tuple-element.13.refs_0_.even_ref.own_even_ref) | copy-start | bytes 3145732
  34.6 102.6 %all-gather.7.cloned.1.call-start = ((), (), s32[]{:S(2)}) async-start(), calls=%async_computation.2 | async-start | bytes 2621440 | tf_op jit(solution)/shard_map/all_gather | solution.py:626
  34.6 22.4 %collective-permute-start.3 = (bf16[512,2048]{1,0:T(8,128)(2,1)S(1)}, bf16[512,2048]{1,0:T(8,128)(2,1)}, u32[]{:S(2)}, u32[]{:S(2)}) collective-permute-start(bf16[512,2048]{1,0:T(8,128)(2,1)S(1)} %copy-done.6), channel_id=1, source_target_pairs={{0,1},{1,0},{2,3},{3,2},{4,5},{5,4},{6,7},{7,6},{8,9},{9,8},{10,11... | collective-permute-start | bytes 6291464 | tf_op jit(solution)/shard_map/ppermute | solution.py:531
  35.7 14.8 %collective-permute-start = (s32[4,64,512]{2,1,0:T(8,128)}, s32[4,64,512]{2,1,0:T(8,128)}, u32[]{:S(2)}, u32[]{:S(2)}) collective-permute-start(s32[4,64,512]{2,1,0:T(8,128)} %get-tuple-element.14.refs_2_), channel_id=1, source_target_pairs={{0,2},{1,3},{4,6},{5,7},{8,10},{9,11},{12,14},{13,15},{16,18},{17,... | collective-permute-start | bytes 1572872 | tf_op jit(solution)/shard_map/ppermute | solution.py:610
  52.5 27.0 %collective-permute-start.2 = (s32[8,64,512]{2,1,0:T(8,128)}, s32[8,64,512]{2,1,0:T(8,128)S(1)}, u32[]{:S(2)}, u32[]{:S(2)}) collective-permute-start(s32[8,64,512]{2,1,0:T(8,128)} %hold.7), channel_id=1, source_target_pairs={{0,2},{1,3},{4,6},{5,7},{8,10},{9,11},{12,14},{13,15},{16,18},{17,... | collective-permute-start | bytes 3145736 | tf_op jit(solution)/shard_map/ppermute | solution.py:610
  56.9 131.2 %reduce-scatter.2.cloned.1.call-start = ((), (), s32[]{:S(2)}) async-start(), calls=%async_computation.1 | async-start | bytes 1310720 | tf_op jit(solution)/shard_map/reduce_scatter | solution.py:652
  60.7 24.7 %collective-permute-start.4 = (bf16[256,2048]{1,0:T(8,128)(2,1)}, bf16[256,2048]{1,0:T(8,128)(2,1)S(1)}, u32[]{:S(2)}, u32[]{:S(2)}) collective-permute-start(bf16[256,2048]{1,0:T(8,128)(2,1)} %get-tuple-element.16.refs_0_), channel_id=1, source_target_pairs={{0,4},{4,0},{1,5},{5,1},{2,6},{6,2},{3,7},{7,3},{8,12},{12,8},{9,1... | collective-permute-start | bytes 3145736 | tf_op jit(solution)/shard_map/ppermute | solution.py:527
  79.5 5.9 %copy-start.2 = (s32[8,64,512]{2,1,0:T(8,128)}, s32[8,64,512]{2,1,0:T(8,128)S(1)}, u32[]{:S(2)}) copy-start(s32[8,64,512]{2,1,0:T(8,128)S(1)} %collective-permute-done.2.refs_1_.even_ref.refs_2_) | copy-start | bytes 3145732
  85.4 1.0 copy-start.3
  86.4 53.4 %collective-permute-start.6 = (s32[4,4,64,512]{3,2,1,0:T(8,128)}, s32[4,4,64,512]{3,2,1,0:T(8,128)}, u32[]{:S(2)}, u32[]{:S(2)}) collective-permute-start(s32[4,4,64,512]{3,2,1,0:T(8,128)} %hold.8.refs_0_), channel_id=1, source_target_pairs={{0,4},{4,0},{1,5},{5,1},{2,6},{6,2},{3,7},{7,3},{8,12},{12,8},{9,1... | collective-permute-start | bytes 6291464 | tf_op jit(solution)/shard_map/ppermute | solution.py:527
  88.8 8.6 %copy-start.10 = (bf16[64,1024]{1,0:T(8,128)(2,1)}, bf16[64,1024]{1,0:T(8,128)(2,1)S(1)}, u32[]{:S(2)}) copy-start(bf16[64,1024]{1,0:T(8,128)(2,1)S(1)} %slice_bitcast_fusion.refs_0_) | copy-start | bytes 393220
  88.8 8.6 %copy-start.5 = (bf16[1024,1024]{1,0:T(8,128)(2,1)S(1)}, bf16[1024,1024]{1,0:T(8,128)(2,1)}, u32[]{:S(2)}) copy-start(bf16[1024,1024]{1,0:T(8,128)(2,1)} %param.6) | copy-start | bytes 6291460
  88.8 31.8 %collective-permute-start.7 = (bf16[64,1024]{1,0:T(8,128)(2,1)S(1)}, bf16[64,1024]{1,0:T(8,128)(2,1)S(1)}, u32[]{:S(2)}, u32[]{:S(2)}) collective-permute-start(bf16[64,1024]{1,0:T(8,128)(2,1)S(1)} %slice_bitcast_fusion.refs_0_), channel_id=1, source_target_pairs={{0,8},{8,16},{16,24},{24,0},{1,9},{9,17},{17,25},{25,1},{2,10},{10... | collective-permute-start | bytes 393224 | tf_op jit(solution)/shard_map/ppermute | solution.py:523
  90.4 30.3 %collective-permute-start.8 = (bf16[64,1024]{1,0:T(8,128)(2,1)S(1)}, bf16[64,1024]{1,0:T(8,128)(2,1)S(1)}, u32[]{:S(2)}, u32[]{:S(2)}) collective-permute-start(bf16[64,1024]{1,0:T(8,128)(2,1)S(1)} %slice_bitcast_fusion.refs_0_), channel_id=1, source_target_pairs={{0,24},{8,0},{16,8},{24,16},{1,25},{9,1},{17,9},{25,17},{2,26},{10... | collective-permute-start | bytes 393224 | tf_op jit(solution)/shard_map/ppermute | solution.py:523
  92.7 28.0 %collective-permute-start.9 = (bf16[64,1024]{1,0:T(8,128)(2,1)S(1)}, bf16[64,1024]{1,0:T(8,128)(2,1)S(1)}, u32[]{:S(2)}, u32[]{:S(2)}) collective-permute-start(bf16[64,1024]{1,0:T(8,128)(2,1)S(1)} %slice_bitcast_fusion.refs_0_), channel_id=1, source_target_pairs={{0,16},{8,24},{16,0},{24,8},{1,17},{9,25},{17,1},{25,9},{2,18},{10... | collective-permute-start | bytes 393224 | tf_op jit(solution)/shard_map/ppermute | solution.py:523
  120.6 2.7 copy-start.1
  120.7 0.6 copy-start.11
  120.7 0.7 copy-start.12
  120.7 0.7 copy-start.13
  123.4 42.9 %collective-permute-start.10 = (s32[4,4,64,512]{3,2,1,0:T(8,128)S(1)}, s32[4,4,64,512]{3,2,1,0:T(8,128)}, u32[]{:S(2)}, u32[]{:S(2)}) collective-permute-start(s32[4,4,64,512]{3,2,1,0:T(8,128)S(1)} %copy-done.1), channel_id=1, source_target_pairs={{0,1},{1,0},{2,3},{3,2},{4,5},{5,4},{6,7},{7,6},{8,9},{9,8},{10,11... | collective-permute-start | bytes 6291464 | tf_op jit(solution)/shard_map/ppermute | solution.py:531
  139.8 1.0 copy-start.8
  139.8 26.5 %collective-permute-start.11 = (s32[4,4,64,512]{3,2,1,0:T(8,128)}, s32[4,4,64,512]{3,2,1,0:T(8,128)}, u32[]{:S(2)}, u32[]{:S(2)}) collective-permute-start(s32[4,4,64,512]{3,2,1,0:T(8,128)} %hold.9.refs_1_), channel_id=1, source_target_pairs={{0,1},{1,0},{2,3},{3,2},{4,5},{5,4},{6,7},{7,6},{8,9},{9,8},{10,11... | collective-permute-start | bytes 6291464 | tf_op jit(solution)/shard_map/ppermute | solution.py:531
  140.8 13.9 %collective-permute-start.12 = (bf16[4,64,1024]{2,1,0:T(8,128)(2,1)S(1)}, bf16[4,64,1024]{2,1,0:T(8,128)(2,1)S(1)}, u32[]{:S(2)}, u32[]{:S(2)}) collective-permute-start(bf16[4,64,1024]{2,1,0:T(8,128)(2,1)S(1)} %copy-done.8), channel_id=1, source_target_pairs={{0,4},{4,0},{1,5},{5,1},{2,6},{6,2},{3,7},{7,3},{8,12},{12,8},{9,1... | collective-permute-start | bytes 1572872 | tf_op jit(solution)/shard_map/ppermute | solution.py:527
  141.3 15.6 %collective-permute-start.13 = (bf16[4,64,1024]{2,1,0:T(8,128)(2,1)S(1)}, bf16[4,64,1024]{2,1,0:T(8,128)(2,1)}, u32[]{:S(2)}, u32[]{:S(2)}) collective-permute-start(bf16[4,64,1024]{2,1,0:T(8,128)(2,1)S(1)} %copy-done.8), channel_id=1, source_target_pairs={{0,1},{1,0},{2,3},{3,2},{4,5},{5,4},{6,7},{7,6},{8,9},{9,8},{10,11... | collective-permute-start | bytes 1572872 | tf_op jit(solution)/shard_map/ppermute | solution.py:531
  154.7 2.3 copy-start.17
  154.7 2.3 collective-permute-start.14
  156.1 81.5 %all-gather.11.cloned.1.call-start = ((), (), s32[]{:S(2)}) async-start(), calls=%async_computation.4 | async-start | bytes 1310720 | tf_op jit(solution)/shard_map/all_gather | solution.py:664
  156.3 53.6 %collective-permute-start.5 = (s32[4,4,64,512]{3,2,1,0:T(8,128)}, s32[4,4,64,512]{3,2,1,0:T(8,128)}, u32[]{:S(2)}, u32[]{:S(2)}) collective-permute-start(s32[4,4,64,512]{3,2,1,0:T(8,128)} %bitcast.46), channel_id=1, source_target_pairs={{0,4},{4,0},{1,5},{5,1},{2,6},{6,2},{3,7},{7,3},{8,12},{12,8},{9,1... | collective-permute-start | bytes 6291464 | tf_op jit(solution)/shard_map/ppermute | solution.py:527
  156.9 53.5 %collective-permute-start.15 = (s32[4,4,64,512]{3,2,1,0:T(8,128)}, s32[4,4,64,512]{3,2,1,0:T(8,128)}, u32[]{:S(2)}, u32[]{:S(2)}) collective-permute-start(s32[4,4,64,512]{3,2,1,0:T(8,128)} %bitcast.47), channel_id=1, source_target_pairs={{0,1},{1,0},{2,3},{3,2},{4,5},{5,4},{6,7},{7,6},{8,9},{9,8},{10,11... | collective-permute-start | bytes 6291464 | tf_op jit(solution)/shard_map/ppermute | solution.py:531
  209.9 4.4 %collective-permute-start.16 = (s32[4,4,64,512]{3,2,1,0:T(8,128)}, s32[4,4,64,512]{3,2,1,0:T(8,128)S(1)}, u32[]{:S(2)}, u32[]{:S(2)}) collective-permute-start(s32[4,4,64,512]{3,2,1,0:T(8,128)} %hold.10.refs_1_), channel_id=1, source_target_pairs={{0,1},{1,0},{2,3},{3,2},{4,5},{5,4},{6,7},{7,6},{8,9},{9,8},{10,11... | collective-permute-start | bytes 6291464 | tf_op jit(solution)/shard_map/ppermute | solution.py:531
  214.3 1.3 copy-start.4
  237.6 25.7 %collective-permute-start.17 = (bf16[4,64,2048]{2,1,0:T(8,128)(2,1)}, bf16[4,64,2048]{2,1,0:T(8,128)(2,1)S(1)}, u32[]{:S(2)}, u32[]{:S(2)}) collective-permute-start(bf16[4,64,2048]{2,1,0:T(8,128)(2,1)} %hold.12.refs_0_), channel_id=1, source_target_pairs={{0,4},{4,0},{1,5},{5,1},{2,6},{6,2},{3,7},{7,3},{8,12},{12,8},{9,1... | collective-permute-start | bytes 3145736 | tf_op jit(solution)/shard_map/ppermute | solution.py:527
  239.2 25.0 %collective-permute-start.18 = (bf16[4,64,2048]{2,1,0:T(8,128)(2,1)}, bf16[4,64,2048]{2,1,0:T(8,128)(2,1)S(1)}, u32[]{:S(2)}, u32[]{:S(2)}) collective-permute-start(bf16[4,64,2048]{2,1,0:T(8,128)(2,1)} %hold.12.refs_0_), channel_id=1, source_target_pairs={{0,1},{1,0},{2,3},{3,2},{4,5},{5,4},{6,7},{7,6},{8,9},{9,8},{10,11... | collective-permute-start | bytes 3145736 | tf_op jit(solution)/shard_map/ppermute | solution.py:531
  263.3 1.0 copy-start.9
  264.2 2.9 collective-permute-start.19
  264.3 2.9 copy-start.15
  267.1 1.0 copy-start.16
Sparse Core Ops, SparseCore 0:
  34.7 47.7 all-gather.8
  84.0 53.0 all-gather.6
  156.2 25.1 reduce-scatter.1
  210.5 26.8 all-gather.10

commit v2 on v1

--- a/solution.py
+++ b/solution.py
@@ -545,6 +545,28 @@
     if after:
         plane[1] = hold(plane[1], after)
     return plane + [other(x) for x in plane]
+
+
+def others_of(line, here):
+    far = line.shape[0]
+    order = jnp.stack([(here - k) % far for k in range(1, far)]).astype(jnp.int32)
+
+    def kernel(order_ref, line_ref, out_ref):
+        out_ref[...] = line_ref[...]
+
+    return pl.pallas_call(
+        kernel,
+        grid_spec=pltpu.PrefetchScalarGridSpec(
+            num_scalar_prefetch=1,
+            grid=(far - 1,),
+            in_specs=[pl.BlockSpec((1, *line.shape[1:]), lambda i, order: (order[i], 0, 0, 0))],
+            out_specs=pl.BlockSpec((1, *line.shape[1:]), lambda i, order: (i, 0, 0, 0)),
+        ),
+        out_shape=jax.ShapeDtypeStruct((far - 1, *line.shape[1:]), line.dtype),
+        compiler_params=pltpu.CompilerParams(vmem_limit_bytes=VMEM),
+        cost_estimate=pl.CostEstimate(flops=1, bytes_accessed=1, transcendentals=0),
+        name="others_of",
+    )(order, line)
 
 
 def add(a, b, after):
@@ -628,6 +650,7 @@
     if split_panel:
         last = wanted = choose(first, even, cuts[0][0], got_odds[0], [last])
         gathered.append(gather(wanted))
+        beside = [near(wanted)]
     else:
         gathered.append(gather(wanted[0]))
     keep = last = own_lost_rows(down_rows, places, span, blocks[0], size, [last])
@@ -635,8 +658,9 @@
         for (start, _), got_odd in list(zip(cuts, got_odds))[1:]:
             last = wanted = choose(first, even, start, got_odd, [last])
             gathered.append(gather(wanted))
+            beside.append(near(wanted))
         got_even = to_one(hold(even, [last]))
-    kept, given = add_halves(keep, got, [last])
+    kept, given = add_halves(keep, got, [last, beside[0]] if split_panel else [last])
     near_got, last = near(given), given
     if split_panel:
         sh, sl = square(turned, [last, got_even, near_got])
@@ -647,21 +671,33 @@
     if split_panel:
         gathered[0] = hold(gathered[0], [near_got, got_even])
     lead_line = join([cross_gram[0, 0]] + lead_turns, [high])
-    lead_parts = spread(lead_line, [])
-    kept = add(kept, near_got, [lead_line, *gathered[1:]])
+    kept = add(kept, near_got, [lead_line, *gathered[1:], *(beside[1:] if split_panel else [])])
     w_own = lax.psum_scatter(kept, "far", scatter_dimension=0, tiled=True)
 
 
-    dh, dl = residual(back, around, high, low, cross_gram, lead_parts, [kept])
-    updated, index = None, 0
-    for line, (start, n) in zip(gathered, cuts):
-        arrays = spread(line, [kept if updated is None else updated])
+    updated, index, panel_places = None, 0, lined
+    if split_panel:
+        places = []
+        for t in (0, 1):
+            places += [member_at(z, (0, t)) for z in range(far)]
+            places += [member_at((here - k) % far, (1, t)) for k in range(far)]
+        panel_places = table(places)
+    for piece, (line, (start, n)) in enumerate(zip(gathered, cuts)):
+        last = kept if updated is None else updated
+        if split_panel:
+            arrays = [line, beside[piece][None], hold(near(others_of(line, here)), [last])]
+            arrays += [other(x) for x in arrays]
+        else:
+            arrays = spread(line, [last])
         part = STEP if n % STEP == 0 else n
         for begin in range(0, n, part):
-            after = [dh] if index == 0 else []
-            updated = update(gram, updated, units * back, lined, high, low, arrays, begin, part, start + begin, after)
+            after = [kept] if index == 0 else [dh] if index == 2 else []
+            updated = update(gram, updated, units * back, panel_places, high, low, arrays, begin, part, start + begin, after)
             if index == 0:
+                lead_parts = spread(lead_line, [updated])
                 w_line = lax.all_gather(hold(w_own, [updated]), "far", axis=0, tiled=False)
+            if index == 1 or n == part:
+                dh, dl = residual(back, around, high, low, cross_gram, lead_parts, [updated])
             if index == 2:
                 w_line = hold(w_line, [updated])
             if index == 3 or n == part:

time: 291 us -> 285 us (0.979)
  waiting for transfers between devices: 59.5 us -> 37.7 us
  Pallas kernels: 165 us -> 173 us
  starting transfers between devices: 25.3 us -> 32 us
    all_gather x2, waiting for transfers between devices: 13.8 us -> 0.01 us  [gather(): return lax.all_gather(piece, 'far', axis=0, tiled=False)]
    pallas_call x0 -> x2, Pallas kernels: none -> 8.37 us  [others_of(): pl.pallas_call(kernel, grid_spec=pltpu.PrefetchScalarGridSpec(num_scalar_...]
    ppermute x5 -> x7, waiting for transfers between devices: 21.4 us -> 15.5 us  [near(): return lax.ppermute(x, 'near', [(0, 1), (1, 0)])]
    ppermute x5 -> x7, starting transfers between devices: 5.71 us -> 11.4 us  [near(): return lax.ppermute(x, 'near', [(0, 1), (1, 0)])]
    ppermute x9 -> x11, waiting for transfers between devices: 6.85 us -> 6.52 us  [other(): return lax.ppermute(x, 'tp', [(0, 1), (1, 0)])]
    unnamed x38 -> x42, local copies, waits for them, and re-layouts: 11.7 us -> 11.5 us
  transfers between devices with their start and end apart: 24 -> 28, of which waited for: 7 -> 8; matrix products, arithmetic and copies ran while one was open for 6% -> 7% of each run, Pallas kernels for 49% -> 53%
where the time goes in v2:
time: 285 us; the launch traced here: 284 us
  Pallas kernels  173 us (61%)
  waiting for transfers between devices  37.7 us (13%)
  starting transfers between devices  32 us (11%)
  local copies, waits for them, and re-layouts  16.7 us (6%)
  between operations  15.5 us (5%)
  other arithmetic  9.17 us (3%)
    pallas_call x4, Pallas kernels, update(): pl.pallas_call(functools.partial(update_kernel, len(words), first_cycle,...  87.1 us
    pallas_call x2, Pallas kernels, own_lost_rows(): pl.pallas_call(own_kernel, grid_spec=pltpu.PrefetchScalarGridSpec(num_sca...  17.3 us
    ppermute x7, waiting for transfers between devices, near(): return lax.ppermute(x, 'near', [(0, 1), (1, 0)])  15.5 us
    ppermute x3, waiting for transfers between devices, per_device(): to_one = lambda x: lax.ppermute(x, 'col', [(0, 1)])  14.9 us
    pallas_call x1, Pallas kernels, rhs_step(): pl.pallas_call(functools.partial(rhs_kernel, len(parts)), out_shape=jax.S...  13.6 us
    unnamed x42, local copies, waits for them, and re-layouts  11.5 us
    pallas_call x1, Pallas kernels, solve(): pl.pallas_call(functools.partial(solve_kernel, pieces), out_shape=[jax.Sh...  11.5 us
    ppermute x7, starting transfers between devices, near(): return lax.ppermute(x, 'near', [(0, 1), (1, 0)])  11.4 us
  transfers between devices with their start and end apart: 28, of which 8 were waited for; matrix products, arithmetic and copies ran while one was open for 7% of the time, Pallas kernels for 53%

profile of v2, /device:TPU:0, one launch (start us, length us, event | category | flops | bytes accessed | tf_op | source)
XLA Modules:
  0.0 284.2 jit_solution(1239132929681202805)
XLA Ops:
  7.2 7.6 %encode_panel.1 = (s32[8,64,512]{2,1,0:T(8,128)}, s32[4,64,512]{2,1,0:T(8,128)}, s32[4,64,512]{2,1,0:T(8,128)}) custom-call(f32[16,1,64,8,1,1024]{5,4,3,2,1,0:T(1,128)} %refs_6_.7), custom_call_target="tpu_custom_call" | custom-call | flops 1 | bytes 1 | tf_op jit(solution)/shard_map/encode_panel/pallas_call | solution.py:115
  14.8 4.9 %collective-permute-start.1 = (s32[4,64,512]{2,1,0:T(8,128)}, s32[4,64,512]{2,1,0:T(8,128)S(1)}, u32[]{:S(2)}, u32[]{:S(2)}) collective-permute-start(s32[4,64,512]{2,1,0:T(8,128)} %get-tuple-element.15.refs_0_), channel_id=1, source_target_pairs={{0,2},{1,3},{4,6},{5,7},{8,10},{9,11},{12,14},{13,15},{16,18},{17,... | collective-permute-start | bytes 1572872 | tf_op jit(solution)/shard_map/ppermute | solution.py:632
  20.3 1.0 copy.23.places_ref
  22.0 1.8 pad_add_fusion.range_ref
  23.9 7.8 %own_lost_rows.2.refs_0_ = bf16[512,2048]{1,0:T(8,128)(2,1)} custom-call(s32[8]{0:T(128)} %stack.197.order_ref, s32[2]{0:T(128)} %pad_add_fusion.range_ref, s32[1024,1]{1,0:T(8,128)} %copy.23.places_ref, bf16[1848,2048]{1,0:T(8,128)(2,1)} %rows_ref.3, s32[8,64,512]{2,1,0:T(8,128)} %get-tuple-element.13.refs_0_.even_ref.own_even_ref), custom_call_target="tpu_custom_call" | custom-call | flops 1 | bytes 1 | tf_op jit(solution)/shard_map/own_lost_rows/pallas_call | solution.py:502
  32.4 2.1 choose.2.refs_0_
  34.6 1.1 collective-permute-start.3
  35.7 3.5 %collective-permute-start = (s32[4,64,512]{2,1,0:T(8,128)}, s32[4,64,512]{2,1,0:T(8,128)}, u32[]{:S(2)}, u32[]{:S(2)}) collective-permute-start(s32[4,64,512]{2,1,0:T(8,128)} %get-tuple-element.14.refs_2_), channel_id=1, source_target_pairs={{0,2},{1,3},{4,6},{5,7},{8,10},{9,11},{12,14},{13,15},{16,18},{17,... | collective-permute-start | bytes 1572872 | tf_op jit(solution)/shard_map/ppermute | solution.py:632
  39.2 3.0 %collective-permute-start.4 = (s32[4,64,512]{2,1,0:T(8,128)}, s32[4,64,512]{2,1,0:T(8,128)}, u32[]{:S(2)}, u32[]{:S(2)}) collective-permute-start(s32[4,64,512]{2,1,0:T(8,128)} %choose.2.refs_0_), channel_id=1, source_target_pairs={{0,4},{4,0},{1,5},{5,1},{2,6},{6,2},{3,7},{7,3},{8,12},{12,8},{9,1... | collective-permute-start | bytes 1572872 | tf_op jit(solution)/shard_map/ppermute | solution.py:527
  42.8 9.5 %own_lost_rows.3.refs_0_.a_ref = bf16[512,2048]{1,0:T(8,128)(2,1)} custom-call(s32[8]{0:T(128)} %stack.189.order_ref, s32[2]{0:T(128)} %pad_add_fusion.range_ref, s32[1024,1]{1,0:T(8,128)} %copy.23.places_ref, bf16[1848,2048]{1,0:T(8,128)(2,1)} %rows_ref.3, s32[4,64,512]{2,1,0:T(8,128)} %choose.2.refs_0_), custom_call_target="tpu_custom_call" | custom-call | flops 1 | bytes 1 | tf_op jit(solution)/shard_map/own_lost_rows/pallas_call | solution.py:502
  52.4 2.0 choose.3.refs_1_.refs_0_
  54.5 1.0 copy.25.refs_0_
  55.5 2.5 collective-permute-start.2
  58.0 3.7 %add_halves.1 = (bf16[256,2048]{1,0:T(8,128)(2,1)}, bf16[256,2048]{1,0:T(8,128)(2,1)}) custom-call(bf16[512,2048]{1,0:T(8,128)(2,1)} %own_lost_rows.3.refs_0_.a_ref, bf16[512,2048]{1,0:T(8,128)(2,1)} %collective-permute-done.3.b_ref, s32[4,64,512]{2,1,0:T(8,128)} %choose.3.refs_1_.refs_0_, s32[4,64,512]{2,1,0:T(8,128)} %collective-permute-done.4.refs_1_), custom_call_target="tpu_custom_call" | custom-call | flops 1 | bytes 1 | tf_op jit(solution)/shard_map/add_halves/pallas_call | solution.py:587
  61.7 3.3 %collective-permute-start.5 = (bf16[256,2048]{1,0:T(8,128)(2,1)}, bf16[256,2048]{1,0:T(8,128)(2,1)S(1)}, u32[]{:S(2)}, u32[]{:S(2)}) collective-permute-start(bf16[256,2048]{1,0:T(8,128)(2,1)} %get-tuple-element.16.refs_0_), channel_id=1, source_target_pairs={{0,4},{4,0},{1,5},{5,1},{2,6},{6,2},{3,7},{7,3},{8,12},{12,8},{9,1... | collective-permute-start | bytes 3145736 | tf_op jit(solution)/shard_map/ppermute | solution.py:527
  65.6 14.9 %collective-permute-done.2.refs_1_.even_ref.refs_2_ = s32[8,64,512]{2,1,0:T(8,128)S(1)} collective-permute-done((s32[8,64,512]{2,1,0:T(8,128)}, s32[8,64,512]{2,1,0:T(8,128)S(1)}, u32[]{:S(2)}, u32[]{:S(2)}) %collective-permute-start.2) | collective-permute-done | bytes 1048608 | tf_op jit(solution)/shard_map/ppermute | solution.py:632
  80.5 7.6 %collective-permute-done.5.refs_2_.refs_1_ = bf16[256,2048]{1,0:T(8,128)(2,1)S(1)} collective-permute-done((bf16[256,2048]{1,0:T(8,128)(2,1)}, bf16[256,2048]{1,0:T(8,128)(2,1)S(1)}, u32[]{:S(2)}, u32[]{:S(2)}) %collective-permute-start.5) | collective-permute-done | bytes 1048608 | tf_op jit(solution)/shard_map/ppermute | solution.py:527
  88.1 1.0 copy-done.4
  89.1 4.1 %others_of.3 = s32[3,4,64,512]{3,2,1,0:T(8,128)} custom-call(s32[3]{0:T(128)} %pad_add_fusion.1.order_ref, s32[4,4,64,512]{3,2,1,0:T(8,128)} %hold.9.line_ref.refs_0_), custom_call_target="tpu_custom_call" | custom-call | flops 1 | bytes 1 | tf_op jit(solution)/shard_map/others_of/pallas_call | solution.py:557
  93.2 1.7 collective-permute-start.8
  95.0 0.9 slice_bitcast_fusion.refs_0_
  95.9 1.6 collective-permute-start.10
  97.5 3.9 %copy.24 = bf16[1024,1024]{0,1:T(8,128)(2,1)} copy(bf16[1024,1024]{1,0:T(8,128)(2,1)} %param.6) | data formatting | bytes 4194304 | tf_op args[1]
  102.0 2.6 abs_reduce_fusion
  106.5 5.1 %collective-permute-start.9 = (bf16[64,1024]{1,0:T(8,128)(2,1)S(1)}, bf16[64,1024]{1,0:T(8,128)(2,1)S(1)}, u32[]{:S(2)}, u32[]{:S(2)}) collective-permute-start(bf16[64,1024]{1,0:T(8,128)(2,1)S(1)} %slice_bitcast_fusion.refs_0_), channel_id=1, source_target_pairs={{0,8},{8,16},{16,24},{24,0},{1,9},{9,17},{17,25},{25,1},{2,10},{10... | collective-permute-start | bytes 393224 | tf_op jit(solution)/shard_map/ppermute | solution.py:523
  111.6 3.4 %fusion.turned_ref = bf16[1024,1024]{1,0:T(8,128)(2,1)} fusion(bf16[1024,1024]{0,1:T(8,128)(2,1)} %copy.24, f32[]{:T(128)S(6)} %select_n.92), kind=kLoop, calls=%fused_computation.1 | loop fusion | flops 3145728 | bytes 4194308 | tf_op jit(solution)/shard_map/transpose | solution.py:621
  115.0 5.9 %square.1 = (bf16[1024,1024]{1,0:T(8,128)(2,1)}, bf16[1024,1024]{1,0:T(8,128)(2,1)}) custom-call(bf16[1024,1024]{1,0:T(8,128)(2,1)} %fusion.turned_ref, bf16[256,2048]{1,0:T(8,128)(2,1)} %get-tuple-element.16.refs_0_, s32[8,64,512]{2,1,0:T(8,128)} %copy-done.3, bf16[256,2048]{1,0:T(8,128)(2,1)} %copy-done.4), custom_call_target="tpu_custom_call" | custom-call | flops 1 | bytes 1 | tf_op jit(solution)/shard_map/square/pallas_call | solution.py:471
  121.0 11.5 %solve.1 = (bf16[1024,1024]{1,0:T(8,128)(2,1)}, bf16[1024,1024]{1,0:T(8,128)(2,1)}) custom-call(f32[1]{0:T(128)} %constant.109.clone.1.factor_ref, f32[1]{0:T(128)} %bitcast.back_ref, s32[1]{0:T(128)} %bitcast.17.first_ref, s32[8,64,512]{2,1,0:T(8,128)} %get-tuple-element.13.refs_0_.even_ref.own_even_ref, s32[8,64,512]{2,1,0:T(8,128)} %copy-done.3, ...), custom_call_target="tpu_custom_call" | custom-call | flops 1 | bytes 1 | tf_op jit(solution)/shard_map/solve/pallas_call | solution.py:247
  133.2 2.0 join.1.refs_2_.refs_0_
  135.2 4.8 %collective-permute-done.6.refs_4_ = s32[4,64,512]{2,1,0:T(8,128)S(1)} collective-permute-done((s32[4,64,512]{2,1,0:T(8,128)S(1)}, s32[4,64,512]{2,1,0:T(8,128)S(1)}, u32[]{:S(2)}, u32[]{:S(2)}) %collective-permute-start.6) | collective-permute-done | bytes 524320 | tf_op jit(solution)/shard_map/ppermute | solution.py:527
  140.0 0.8 copy-done.7
  140.8 2.6 add.317.refs_1_.refs_7_
  143.5 1.1 copy-done.2
  145.9 1.5 collective-permute-start.18
  147.3 4.3 %others_of.2 = s32[3,4,64,512]{3,2,1,0:T(8,128)} custom-call(s32[3]{0:T(128)} %pad_add_fusion.1.order_ref, s32[4,4,64,512]{3,2,1,0:T(8,128)} %bitcast.50), custom_call_target="tpu_custom_call" | custom-call | flops 1 | bytes 1 | tf_op jit(solution)/shard_map/others_of/pallas_call | solution.py:557
  152.4 21.7 %trailing_update.4.refs_7_.refs_1_ = f32[16,1,64,8,1,1024]{5,4,3,2,1,0:T(1,128)} custom-call(f32[1]{0:T(128)S(6)} %mul_broadcast_in_dim.2.factor_ref, s32[16]{0:T(128)} %stack.184.places_ref, bf16[1024,1024]{1,0:T(8,128)(2,1)} %get-tuple-element.19.refs_4_.high_ref, bf16[1024,1024]{1,0:T(8,128)(2,1)} %get-tuple-element.20.low_ref, ...), custom_call_target="tpu_custom_call" | custom-call | flops 17179869184 | bytes 1 | tf_op jit(solution)/shard_map/trailing_update/pallas_call | solution.py:371
  174.2 21.8 %trailing_update.5.refs_1_.refs_4_.refs_7_ = f32[16,1,64,8,1,1024]{5,4,3,2,1,0:T(1,128)} custom-call(f32[1]{0:T(128)S(6)} %mul_broadcast_in_dim.2.factor_ref, s32[16]{0:T(128)} %stack.184.places_ref, bf16[1024,1024]{1,0:T(8,128)(2,1)} %get-tuple-element.19.refs_4_.high_ref, ...), custom_call_target="tpu_custom_call", output_to_operand_aliasing={{}: (11, {})} | custom-call | flops 17179869184 | bytes 1 | tf_op jit(solution)/shard_map/trailing_update/pallas_call | solution.py:371
  197.9 3.2 %collective-permute-done.19.refs_2_ = bf16[4,64,1024]{2,1,0:T(8,128)(2,1)} collective-permute-done((bf16[4,64,1024]{2,1,0:T(8,128)(2,1)S(1)}, bf16[4,64,1024]{2,1,0:T(8,128)(2,1)}, u32[]{:S(2)}, u32[]{:S(2)}) %collective-permute-start.19) | collective-permute-done | bytes 524320 | tf_op jit(solution)/shard_map/ppermute | solution.py:531
  201.2 1.1 collective-permute-done.20.refs_3_
  202.2 9.4 %residual.1 = (bf16[1024,1024]{1,0:T(8,128)(2,1)}, bf16[1024,1024]{1,0:T(8,128)(2,1)}) custom-call(f32[1]{0:T(128)} %bitcast.back_ref, s32[16]{0:T(128)} %stack.210.places_ref, bf16[1024,1024]{1,0:T(8,128)(2,1)} %get-tuple-element.19.refs_4_.high_ref, bf16[1024,1024]{1,0:T(8,128)(2,1)} %get-tuple-element.20.low_ref, bf16[16,1,64,1024]{3,2,1,0:T(8,128)(2,1)} %cross_ref.1, ...), custom_call_target="tpu_custom_call" | custom-call | flops 8999999488 | bytes 1 | tf_op jit(solution)/shard_map/residual/pallas_call | solution.py:420
  211.6 21.8 %trailing_update.6.refs_7_.refs_1_ = f32[16,1,64,8,1,1024]{5,4,3,2,1,0:T(1,128)} custom-call(f32[1]{0:T(128)S(6)} %mul_broadcast_in_dim.2.factor_ref, s32[16]{0:T(128)} %stack.184.places_ref, bf16[1024,1024]{1,0:T(8,128)(2,1)} %get-tuple-element.19.refs_4_.high_ref, bf16[1024,1024]{1,0:T(8,128)(2,1)} %get-tuple-element.20.low_ref, ...), custom_call_target="tpu_custom_call", output_to_operand_aliasing={{}: (11, {})} | custom-call | flops 17179869184 | bytes 1 | tf_op jit(solution)/shard_map/trailing_update/pallas_call | solution.py:371
  233.5 0.8 collective-permute-start.21
  234.3 21.8 %trailing_update.7.refs_1_.refs_4_ = f32[16,1,64,8,1,1024]{5,4,3,2,1,0:T(1,128)} custom-call(f32[1]{0:T(128)S(6)} %mul_broadcast_in_dim.2.factor_ref, s32[16]{0:T(128)} %stack.184.places_ref, bf16[1024,1024]{1,0:T(8,128)(2,1)} %get-tuple-element.19.refs_4_.high_ref, bf16[1024,1024]{1,0:T(8,128)(2,1)} %get-tuple-element.20.low_ref, ...), custom_call_target="tpu_custom_call", output_to_operand_aliasing={{}: (11, {})} | custom-call | flops 17179869184 | bytes 1 | tf_op jit(solution)/shard_map/trailing_update/pallas_call | solution.py:371
  256.1 3.1 %collective-permute-done.21.refs_0_ = bf16[4,64,2048]{2,1,0:T(8,128)(2,1)S(1)} collective-permute-done((bf16[4,64,2048]{2,1,0:T(8,128)(2,1)}, bf16[4,64,2048]{2,1,0:T(8,128)(2,1)S(1)}, u32[]{:S(2)}, u32[]{:S(2)}) %collective-permute-start.21) | collective-permute-done | bytes 1048608 | tf_op jit(solution)/shard_map/ppermute | solution.py:527
  259.2 1.0 copy-done.12
  260.9 2.2 collective-permute-done.23.refs_3_
  263.1 1.0 copy-done.19
  264.1 13.6 %rhs_step.1 = f32[16,1,64,2048]{3,2,1,0:T(8,128)} custom-call(s32[16]{0:T(128)} %stack.211.places_ref, bf16[1024,1024]{1,0:T(8,128)(2,1)} %get-tuple-element.22.refs_8_.dh_ref, bf16[1024,1024]{1,0:T(8,128)(2,1)} %get-tuple-element.23.dl_ref, bf16[4,64,2048]{2,1,0:T(8,128)(2,1)} %hold.14.refs_0_, bf16[4,64,2048]{2,1,0:T(8,128)(2,1)} %hold.15.refs_1_, ...), custom_call_target="tpu_custom_call" | custom-call | flops 14000000000 | bytes 1 | tf_op jit(solution)/shard_map/rhs_step/pallas_call | solution.py:449
  (92 shorter events, 10.0 us)
Async XLA Ops:
  7.2 12.5 %copy-start.17 = (s32[1024]{0:T(1024)S(1)}, s32[1024]{0:T(1024)}, u32[]{:S(2)}) copy-start(s32[1024]{0:T(1024)} %param.9) | copy-start | bytes 12292
  7.2 80.9 %all-gather.9.cloned.1.call-start = ((), (), s32[]{:S(2)}) async-start(), calls=%async_computation.3 | async-start | bytes 2621440 | tf_op jit(solution)/shard_map/all_gather | solution.py:648
  14.8 16.9 %collective-permute-start.1 = (s32[4,64,512]{2,1,0:T(8,128)}, s32[4,64,512]{2,1,0:T(8,128)S(1)}, u32[]{:S(2)}, u32[]{:S(2)}) collective-permute-start(s32[4,64,512]{2,1,0:T(8,128)} %get-tuple-element.15.refs_0_), channel_id=1, source_target_pairs={{0,2},{1,3},{4,6},{5,7},{8,10},{9,11},{12,14},{13,15},{16,18},{17,... | collective-permute-start | bytes 1572872 | tf_op jit(solution)/shard_map/ppermute | solution.py:632
  31.7 0.8 copy-start.11
  32.4 2.2 copy-start.6
  34.5 105.5 %all-gather.7.cloned.1.call-start = ((), (), s32[]{:S(2)}) async-start(), calls=%async_computation.2 | async-start | bytes 2621440 | tf_op jit(solution)/shard_map/all_gather | solution.py:648
  34.6 23.4 %collective-permute-start.3 = (bf16[512,2048]{1,0:T(8,128)(2,1)S(1)}, bf16[512,2048]{1,0:T(8,128)(2,1)}, u32[]{:S(2)}, u32[]{:S(2)}) collective-permute-start(bf16[512,2048]{1,0:T(8,128)(2,1)S(1)} %copy-done.6), channel_id=1, source_target_pairs={{0,1},{1,0},{2,3},{3,2},{4,5},{5,4},{6,7},{7,6},{8,9},{9,8},{10,11... | collective-permute-start | bytes 6291464 | tf_op jit(solution)/shard_map/ppermute | solution.py:531
  35.7 16.7 %collective-permute-start = (s32[4,64,512]{2,1,0:T(8,128)}, s32[4,64,512]{2,1,0:T(8,128)}, u32[]{:S(2)}, u32[]{:S(2)}) collective-permute-start(s32[4,64,512]{2,1,0:T(8,128)} %get-tuple-element.14.refs_2_), channel_id=1, source_target_pairs={{0,2},{1,3},{4,6},{5,7},{8,10},{9,11},{12,14},{13,15},{16,18},{17,... | collective-permute-start | bytes 1572872 | tf_op jit(solution)/shard_map/ppermute | solution.py:632
  39.2 18.7 %collective-permute-start.4 = (s32[4,64,512]{2,1,0:T(8,128)}, s32[4,64,512]{2,1,0:T(8,128)}, u32[]{:S(2)}, u32[]{:S(2)}) collective-permute-start(s32[4,64,512]{2,1,0:T(8,128)} %choose.2.refs_0_), channel_id=1, source_target_pairs={{0,4},{4,0},{1,5},{5,1},{2,6},{6,2},{3,7},{7,3},{8,12},{12,8},{9,1... | collective-permute-start | bytes 1572872 | tf_op jit(solution)/shard_map/ppermute | solution.py:527
  52.4 2.1 copy-start.1
  54.4 119.8 %reduce-scatter.2.cloned.1.call-start = ((), (), s32[]{:S(2)}) async-start(), calls=%async_computation.1 | async-start | bytes 1310720 | tf_op jit(solution)/shard_map/reduce_scatter | solution.py:675
  55.5 25.0 %collective-permute-start.2 = (s32[8,64,512]{2,1,0:T(8,128)}, s32[8,64,512]{2,1,0:T(8,128)S(1)}, u32[]{:S(2)}, u32[]{:S(2)}) collective-permute-start(s32[8,64,512]{2,1,0:T(8,128)} %hold.8), channel_id=1, source_target_pairs={{0,2},{1,3},{4,6},{5,7},{8,10},{9,11},{12,14},{13,15},{16,18},{17,... | collective-permute-start | bytes 3145736 | tf_op jit(solution)/shard_map/ppermute | solution.py:632
  61.7 26.4 %collective-permute-start.5 = (bf16[256,2048]{1,0:T(8,128)(2,1)}, bf16[256,2048]{1,0:T(8,128)(2,1)S(1)}, u32[]{:S(2)}, u32[]{:S(2)}) collective-permute-start(bf16[256,2048]{1,0:T(8,128)(2,1)} %get-tuple-element.16.refs_0_), channel_id=1, source_target_pairs={{0,4},{4,0},{1,5},{5,1},{2,6},{6,2},{3,7},{7,3},{8,12},{12,8},{9,1... | collective-permute-start | bytes 3145736 | tf_op jit(solution)/shard_map/ppermute | solution.py:527
  80.5 7.6 %copy-start.3 = (s32[8,64,512]{2,1,0:T(8,128)}, s32[8,64,512]{2,1,0:T(8,128)S(1)}, u32[]{:S(2)}) copy-start(s32[8,64,512]{2,1,0:T(8,128)S(1)} %collective-permute-done.2.refs_1_.even_ref.refs_2_) | copy-start | bytes 3145732
  88.1 1.0 copy-start.4
  93.2 50.2 %collective-permute-start.8 = (s32[3,4,64,512]{3,2,1,0:T(8,128)}, s32[3,4,64,512]{3,2,1,0:T(8,128)S(1)}, u32[]{:S(2)}, u32[]{:S(2)}) collective-permute-start(s32[3,4,64,512]{3,2,1,0:T(8,128)} %others_of.3), channel_id=1, source_target_pairs={{0,4},{4,0},{1,5},{5,1},{2,6},{6,2},{3,7},{7,3},{8,12},{12,8},{9,1... | collective-permute-start | bytes 4718600 | tf_op jit(solution)/shard_map/ppermute | solution.py:527
  95.9 10.7 %copy-start.13 = (bf16[64,1024]{1,0:T(8,128)(2,1)}, bf16[64,1024]{1,0:T(8,128)(2,1)S(1)}, u32[]{:S(2)}) copy-start(bf16[64,1024]{1,0:T(8,128)(2,1)S(1)} %slice_bitcast_fusion.refs_0_) | copy-start | bytes 393220
  95.9 5.6 %copy-start.5 = (s32[4,64,512]{2,1,0:T(8,128)S(1)}, s32[4,64,512]{2,1,0:T(8,128)}, u32[]{:S(2)}) copy-start(s32[4,64,512]{2,1,0:T(8,128)} %choose.3.refs_1_.refs_0_) | copy-start | bytes 1572868
  95.9 10.7 %collective-permute-start.10 = (bf16[64,1024]{1,0:T(8,128)(2,1)S(1)}, bf16[64,1024]{1,0:T(8,128)(2,1)S(1)}, u32[]{:S(2)}, u32[]{:S(2)}) collective-permute-start(bf16[64,1024]{1,0:T(8,128)(2,1)S(1)} %slice_bitcast_fusion.refs_0_), channel_id=1, source_target_pairs={{0,24},{8,0},{16,8},{24,16},{1,25},{9,1},{17,9},{25,17},{2,26},{10... | collective-permute-start | bytes 393224 | tf_op jit(solution)/shard_map/ppermute | solution.py:523
  97.5 35.0 %collective-permute-start.11 = (bf16[64,1024]{1,0:T(8,128)(2,1)S(1)}, bf16[64,1024]{1,0:T(8,128)(2,1)S(1)}, u32[]{:S(2)}, u32[]{:S(2)}) collective-permute-start(bf16[64,1024]{1,0:T(8,128)(2,1)S(1)} %slice_bitcast_fusion.refs_0_), channel_id=1, source_target_pairs={{0,16},{8,24},{16,0},{24,8},{1,17},{9,25},{17,1},{25,9},{2,18},{10... | collective-permute-start | bytes 393224 | tf_op jit(solution)/shard_map/ppermute | solution.py:523
  101.5 38.5 %collective-permute-start.6 = (s32[4,64,512]{2,1,0:T(8,128)S(1)}, s32[4,64,512]{2,1,0:T(8,128)S(1)}, u32[]{:S(2)}, u32[]{:S(2)}) collective-permute-start(s32[4,64,512]{2,1,0:T(8,128)S(1)} %copy-done.5), channel_id=1, source_target_pairs={{0,4},{4,0},{1,5},{5,1},{2,6},{6,2},{3,7},{7,3},{8,12},{12,8},{9,1... | collective-permute-start | bytes 1572872 | tf_op jit(solution)/shard_map/ppermute | solution.py:527
  102.0 50.2 %collective-permute-start.12 = (s32[4,4,64,512]{3,2,1,0:T(8,128)}, s32[4,4,64,512]{3,2,1,0:T(8,128)}, u32[]{:S(2)}, u32[]{:S(2)}) collective-permute-start(s32[4,4,64,512]{3,2,1,0:T(8,128)} %hold.9.line_ref.refs_0_), channel_id=1, source_target_pairs={{0,1},{1,0},{2,3},{3,2},{4,5},{5,4},{6,7},{7,6},{8,9},{9,8},{10,11... | collective-permute-start | bytes 6291464 | tf_op jit(solution)/shard_map/ppermute | solution.py:531
  106.5 8.5 %copy-start.14 = (bf16[64,1024]{1,0:T(8,128)(2,1)}, bf16[64,1024]{1,0:T(8,128)(2,1)S(1)}, u32[]{:S(2)}) copy-start(bf16[64,1024]{1,0:T(8,128)(2,1)S(1)} %collective-permute-done.10.refs_2_) | copy-start | bytes 393220
  106.5 26.0 %collective-permute-start.9 = (bf16[64,1024]{1,0:T(8,128)(2,1)S(1)}, bf16[64,1024]{1,0:T(8,128)(2,1)S(1)}, u32[]{:S(2)}, u32[]{:S(2)}) collective-permute-start(bf16[64,1024]{1,0:T(8,128)(2,1)S(1)} %slice_bitcast_fusion.refs_0_), channel_id=1, source_target_pairs={{0,8},{8,16},{16,24},{24,0},{1,9},{9,17},{17,25},{25,1},{2,10},{10... | collective-permute-start | bytes 393224 | tf_op jit(solution)/shard_map/ppermute | solution.py:523
  132.5 0.6 copy-start.15
  132.5 0.7 copy-start.16
  140.0 0.8 copy-start.7
  143.4 2.4 copy-start.9
  143.4 1.1 copy-start.2
  144.6 7.6 %collective-permute-start.14 = (s32[3,4,64,512]{3,2,1,0:T(8,128)}, s32[3,4,64,512]{3,2,1,0:T(8,128)}, u32[]{:S(2)}, u32[]{:S(2)}) collective-permute-start(s32[3,4,64,512]{3,2,1,0:T(8,128)} %hold.10.refs_2_), channel_id=1, source_target_pairs={{0,1},{1,0},{2,3},{3,2},{4,5},{5,4},{6,7},{7,6},{8,9},{9,8},{10,11... | collective-permute-start | bytes 4718600 | tf_op jit(solution)/shard_map/ppermute | solution.py:531
  144.6 7.0 %collective-permute-start.13 = (s32[1,4,64,512]{3,2,1,0:T(8,128)}, s32[1,4,64,512]{3,2,1,0:T(8,128)S(1)}, u32[]{:S(2)}, u32[]{:S(2)}) collective-permute-start(s32[1,4,64,512]{3,2,1,0:T(8,128)} %bitcast.36.refs_1_), channel_id=1, source_target_pairs={{0,1},{1,0},{2,3},{3,2},{4,5},{5,4},{6,7},{7,6},{8,9},{9,8},{10,11... | collective-permute-start | bytes 1572872 | tf_op jit(solution)/shard_map/ppermute | solution.py:531
  145.1 6.4 %copy-start = (s32[16,64,512]{2,1,0:T(8,128)S(1)}, s32[16,64,512]{2,1,0:T(8,128)}, u32[]{:S(2)}) copy-start(s32[16,64,512]{2,1,0:T(8,128)} %all-gather.7.cloned.1.call-done) | copy-start | bytes 6291460
  145.1 88.3 %all-gather.11.cloned.1.call-start = ((), (), s32[]{:S(2)}) async-start(), calls=%async_computation.4 | async-start | bytes 1310720 | tf_op jit(solution)/shard_map/all_gather | solution.py:698
  145.9 28.3 %collective-permute-start.18 = (bf16[4,64,1024]{2,1,0:T(8,128)(2,1)S(1)}, bf16[4,64,1024]{2,1,0:T(8,128)(2,1)}, u32[]{:S(2)}, u32[]{:S(2)}) collective-permute-start(bf16[4,64,1024]{2,1,0:T(8,128)(2,1)S(1)} %copy-done.9), channel_id=1, source_target_pairs={{0,4},{4,0},{1,5},{5,1},{2,6},{6,2},{3,7},{7,3},{8,12},{12,8},{9,1... | collective-permute-start | bytes 1572872 | tf_op jit(solution)/shard_map/ppermute | solution.py:527
  151.6 60.0 %collective-permute-start.15 = (s32[4,4,64,512]{3,2,1,0:T(8,128)S(1)}, s32[4,4,64,512]{3,2,1,0:T(8,128)}, u32[]{:S(2)}, u32[]{:S(2)}) collective-permute-start(s32[4,4,64,512]{3,2,1,0:T(8,128)S(1)} %bitcast.53), channel_id=1, source_target_pairs={{0,1},{1,0},{2,3},{3,2},{4,5},{5,4},{6,7},{7,6},{8,9},{9,8},{10,11... | collective-permute-start | bytes 6291464 | tf_op jit(solution)/shard_map/ppermute | solution.py:531
  151.6 0.8 copy-start.10
  151.6 44.4 %collective-permute-start.7 = (s32[3,4,64,512]{3,2,1,0:T(8,128)}, s32[3,4,64,512]{3,2,1,0:T(8,128)}, u32[]{:S(2)}, u32[]{:S(2)}) collective-permute-start(s32[3,4,64,512]{3,2,1,0:T(8,128)} %others_of.2), channel_id=1, source_target_pairs={{0,4},{4,0},{1,5},{5,1},{2,6},{6,2},{3,7},{7,3},{8,12},{12,8},{9,1... | collective-permute-start | bytes 4718600 | tf_op jit(solution)/shard_map/ppermute | solution.py:527
  196.0 1.8 copy-start.8
  196.0 15.6 %collective-permute-start.17 = (s32[3,4,64,512]{3,2,1,0:T(8,128)}, s32[3,4,64,512]{3,2,1,0:T(8,128)}, u32[]{:S(2)}, u32[]{:S(2)}) collective-permute-start(s32[3,4,64,512]{3,2,1,0:T(8,128)} %hold.11.refs_2_), channel_id=1, source_target_pairs={{0,1},{1,0},{2,3},{3,2},{4,5},{5,4},{6,7},{7,6},{8,9},{9,8},{10,11... | collective-permute-start | bytes 4718600 | tf_op jit(solution)/shard_map/ppermute | solution.py:531
  196.6 4.5 %collective-permute-start.19 = (bf16[4,64,1024]{2,1,0:T(8,128)(2,1)S(1)}, bf16[4,64,1024]{2,1,0:T(8,128)(2,1)}, u32[]{:S(2)}, u32[]{:S(2)}) collective-permute-start(bf16[4,64,1024]{2,1,0:T(8,128)(2,1)S(1)} %copy-done.9), channel_id=1, source_target_pairs={{0,1},{1,0},{2,3},{3,2},{4,5},{5,4},{6,7},{7,6},{8,9},{9,8},{10,11... | collective-permute-start | bytes 1572872 | tf_op jit(solution)/shard_map/ppermute | solution.py:531
  196.7 5.5 %collective-permute-start.20 = (bf16[4,64,1024]{2,1,0:T(8,128)(2,1)}, bf16[4,64,1024]{2,1,0:T(8,128)(2,1)}, u32[]{:S(2)}, u32[]{:S(2)}) collective-permute-start(bf16[4,64,1024]{2,1,0:T(8,128)(2,1)} %hold.12.refs_1_), channel_id=1, source_target_pairs={{0,1},{1,0},{2,3},{3,2},{4,5},{5,4},{6,7},{7,6},{8,9},{9,8},{10,11... | collective-permute-start | bytes 1572872 | tf_op jit(solution)/shard_map/ppermute | solution.py:531
  197.8 13.8 %collective-permute-start.16 = (s32[1,4,64,512]{3,2,1,0:T(8,128)S(1)}, s32[1,4,64,512]{3,2,1,0:T(8,128)}, u32[]{:S(2)}, u32[]{:S(2)}) collective-permute-start(s32[1,4,64,512]{3,2,1,0:T(8,128)S(1)} %bitcast.56), channel_id=1, source_target_pairs={{0,1},{1,0},{2,3},{3,2},{4,5},{5,4},{6,7},{7,6},{8,9},{9,8},{10,11... | collective-permute-start | bytes 1572872 | tf_op jit(solution)/shard_map/ppermute | solution.py:531
  233.5 25.7 %collective-permute-start.21 = (bf16[4,64,2048]{2,1,0:T(8,128)(2,1)}, bf16[4,64,2048]{2,1,0:T(8,128)(2,1)S(1)}, u32[]{:S(2)}, u32[]{:S(2)}) collective-permute-start(bf16[4,64,2048]{2,1,0:T(8,128)(2,1)} %hold.14.refs_0_), channel_id=1, source_target_pairs={{0,4},{4,0},{1,5},{5,1},{2,6},{6,2},{3,7},{7,3},{8,12},{12,8},{9,1... | collective-permute-start | bytes 3145736 | tf_op jit(solution)/shard_map/ppermute | solution.py:527
  234.3 26.6 %collective-permute-start.22 = (bf16[4,64,2048]{2,1,0:T(8,128)(2,1)}, bf16[4,64,2048]{2,1,0:T(8,128)(2,1)S(1)}, u32[]{:S(2)}, u32[]{:S(2)}) collective-permute-start(bf16[4,64,2048]{2,1,0:T(8,128)(2,1)} %hold.14.refs_0_), channel_id=1, source_target_pairs={{0,1},{1,0},{2,3},{3,2},{4,5},{5,4},{6,7},{7,6},{8,9},{9,8},{10,11... | collective-permute-start | bytes 3145736 | tf_op jit(solution)/shard_map/ppermute | solution.py:531
  259.2 1.0 copy-start.12
  260.2 2.9 %collective-permute-start.23 = (bf16[4,64,2048]{2,1,0:T(8,128)(2,1)}, bf16[4,64,2048]{2,1,0:T(8,128)(2,1)S(1)}, u32[]{:S(2)}, u32[]{:S(2)}) collective-permute-start(bf16[4,64,2048]{2,1,0:T(8,128)(2,1)} %hold.15.refs_1_), channel_id=1, source_target_pairs={{0,1},{1,0},{2,3},{3,2},{4,5},{5,4},{6,7},{7,6},{8,9},{9,8},{10,11... | collective-permute-start | bytes 3145736 | tf_op jit(solution)/shard_map/ppermute | solution.py:531
  260.9 2.2 copy-start.18
  263.1 1.0 copy-start.19
Sparse Core Ops, SparseCore 0:
  34.7 47.7 all-gather.8
  84.0 55.7 all-gather.6
  145.3 25.0 reduce-scatter.1
  198.0 25.5 all-gather.10
